TPU v7x, 32 devices: a whole 2x2x4 slice. The times are simulated.
32 devices in a mesh: dp: 2 (over y), expert: 16 (over z, x, core).
Axes of the slice: x: 2, y: 2, z: 4, core: 2. Of those that a mesh axis runs over, the one named last changes fastest.
Arguments:
- tokens: bfloat16 [128, 4096], P('expert', 'dp'), may hold values from -6 to 6
- expert_ids: int32 [128, 8], P('expert'), may hold values from 0 to 15, all different within a row; in each aligned block of 8 rows (0 to 7, 8 to 15, ...) at most 8 rows name the same one
- route_weights: float32 [128, 8], P('expert'), may hold values from 0.2 to 1
- w_gate: bfloat16 [16, 4096, 768], P('expert', 'dp'), may hold values from -0.09375 to 0.09375
- w_up: bfloat16 [16, 4096, 768], P('expert', 'dp'), may hold values from -0.09375 to 0.09375
- w_down: bfloat16 [16, 768, 4096], P('expert', None, 'dp'), may hold values from -0.21875 to 0.21875
- grad_out: bfloat16 [128, 4096], P('expert', 'dp'), may hold values from -6 to 6
Outputs:
- layer_out: bfloat16 [128, 4096], P('expert', 'dp')
- input_grad: bfloat16 [128, 4096], P('expert', 'dp')
- gate_weight_grad: bfloat16 [16, 4096, 768], P('expert', 'dp')
- up_weight_grad: bfloat16 [16, 4096, 768], P('expert', 'dp')
- down_weight_grad: bfloat16 [16, 768, 4096], P('expert', None, 'dp')
Inputs may be any that keep to these rules, and one draw needn't show every extreme that they name: `expert_ids`: among the 8 tokens of one block no expert is named more than 8 times, and in some block some expert is named exactly 8 times; a token names 8 different experts.
All inputs are finite; a program needn't handle non-finite values.
Results may differ from a plain program's by a relative error of at most 0.028.
Values may be sent and summed in bfloat16 or wider, within the bound.
A program may use at most 64 MiB of HBM per device.

v0:
```python
import jax
import jax.numpy as jnp
from jax import lax
from jax.sharding import PartitionSpec as P


def slot_table(id_block, experts, capacity):
    flat_ids = id_block.reshape(-1)
    onehot = (flat_ids[:, None] == jnp.arange(experts, dtype=jnp.int32)[None, :]).astype(jnp.int32)
    before = jnp.cumsum(onehot, axis=0) - onehot
    slot_index = jnp.sum(before * onehot, axis=1)
    target = flat_ids * capacity + slot_index
    row_index = jnp.arange(experts * capacity, dtype=jnp.int32)
    return (row_index[:, None] == target[None, :]).astype(jnp.bfloat16)


def gate_grads(hidden_grad, gate, up_value):
    sigmoid_gate = jax.nn.sigmoid(gate)
    silu_gate = gate * sigmoid_gate
    gate_grad = (
        hidden_grad * up_value * sigmoid_gate * (1.0 + gate * (1.0 - sigmoid_gate))
    ).astype(jnp.bfloat16)
    up_grad = (hidden_grad * silu_gate).astype(jnp.bfloat16)
    return (gate_grad, up_grad)


def contract_rows(left, right):
    return lax.dot_general(
        left, right, (((0,), (0,)), ((), ())), preferred_element_type=jnp.float32
    )


def contract_cols(left, right):
    return lax.dot_general(
        left, right, (((1,), (1,)), ((), ())), preferred_element_type=jnp.float32
    )


def local(tokens, expert_ids, route_weights, w_gate, w_up, w_down, grad_out):
    tok_rows = tokens.shape[0]
    slices = tokens.shape[1]
    top_count = expert_ids.shape[1]
    experts = lax.axis_size("expert")
    capacity = min(tok_rows, 3 * tok_rows * top_count // experts)
    table = slot_table(expert_ids, experts, capacity)
    weight_flat = route_weights.reshape(-1)
    token_replicas = jnp.repeat(tokens, top_count, axis=0)
    grad_rep = (
        jnp.repeat(grad_out, top_count, axis=0).astype(jnp.float32) * weight_flat[:, None]
    ).astype(jnp.bfloat16)
    dispatch_token_rows = jnp.dot(table, token_replicas, preferred_element_type=jnp.float32).astype(
        jnp.bfloat16
    )
    dispatch_gradients = jnp.dot(table, grad_rep, preferred_element_type=jnp.float32).astype(
        jnp.bfloat16
    )
    dispatch_token_rows = dispatch_token_rows.reshape(experts, capacity, slices)
    dispatch_gradients = dispatch_gradients.reshape(experts, capacity, slices)
    expert_in, expert_grad = (
        lax.all_to_all(dispatch_token_rows, "expert", split_axis=0, concat_axis=0, tiled=True),
        lax.all_to_all(dispatch_gradients, "expert", split_axis=0, concat_axis=0, tiled=True),
    )
    expert_in = expert_in.reshape(-1, slices)
    expert_grad = expert_grad.reshape(-1, slices)
    gate_matrix = w_gate[0]
    up_matrix = w_up[0]
    down_matrix = w_down[0]
    gate_part = jnp.dot(expert_in, gate_matrix, preferred_element_type=jnp.float32)
    up_part = jnp.dot(expert_in, up_matrix, preferred_element_type=jnp.float32)
    gate, up_value = (
        lax.psum(gate_part.astype(jnp.bfloat16), "dp").astype(jnp.float32),
        lax.psum(up_part.astype(jnp.bfloat16), "dp").astype(jnp.float32),
    )
    hidden = (gate * jax.nn.sigmoid(gate) * up_value).astype(jnp.bfloat16)
    expert_out = jnp.dot(hidden, down_matrix, preferred_element_type=jnp.float32).astype(
        jnp.bfloat16
    )
    out_blocks = expert_out.reshape(experts, capacity, slices)
    grad_part = contract_cols(expert_grad, down_matrix)
    hidden_grad = lax.psum(grad_part.astype(jnp.bfloat16), "dp").astype(jnp.float32)
    gate_grad, up_grad = gate_grads(hidden_grad, gate, up_value)
    down_grad = contract_rows(hidden, expert_grad).astype(jnp.bfloat16)
    gate_weight = contract_rows(expert_in, gate_grad).astype(jnp.bfloat16)
    up_weight = contract_rows(expert_in, up_grad).astype(jnp.bfloat16)
    input_rows = (contract_cols(gate_grad, gate_matrix) + contract_cols(up_grad, up_matrix)).astype(
        jnp.bfloat16
    )
    input_blocks = input_rows.reshape(experts, capacity, slices)
    out_back, input_back = (
        lax.all_to_all(out_blocks, "expert", split_axis=0, concat_axis=0, tiled=True),
        lax.all_to_all(input_blocks, "expert", split_axis=0, concat_axis=0, tiled=True),
    )
    backward_output = contract_rows(table, out_back.reshape(-1, slices)).reshape(
        tok_rows, top_count, slices
    )
    backward_input = contract_rows(table, input_back.reshape(-1, slices)).reshape(
        tok_rows, top_count, slices
    )
    layer_out = jnp.sum(backward_output * route_weights[:, :, None], axis=1).astype(jnp.bfloat16)
    input_grad = jnp.sum(backward_input, axis=1).astype(jnp.bfloat16)
    return (layer_out, input_grad, gate_weight[None], up_weight[None], down_grad[None])


def solution(mesh):
    return jax.shard_map(
        local,
        mesh=mesh,
        in_specs=(
            P("expert", "dp"),
            P("expert", None),
            P("expert", None),
            P("expert", "dp", None),
            P("expert", "dp", None),
            P("expert", None, "dp"),
            P("expert", "dp"),
        ),
        out_specs=(
            P("expert", "dp"),
            P("expert", "dp"),
            P("expert", "dp", None),
            P("expert", "dp", None),
            P("expert", None, "dp"),
        ),
        check_vma=False,
    )
```

profile of v0, /device:TPU:0, one launch (start us, length us, event | category | flops | bytes accessed | tf_op | source)
XLA Modules:
  0.0 134.2 jit_solution(7728857750771198582)
XLA Ops:
  7.2 0.0 copy-start
  7.2 0.9 reshape.93
  8.1 0.1 fusion.67
  8.2 0.1 reduce_window_sum.11
  8.3 0.2 select_reduce_fusion
  8.5 1.8 %fusion.24 = bf16[16,8,2048]{2,1,0:T(8,128)(2,1)} fusion(bf16[8,2048]{1,0:T(8,128)(2,1)} %param.7, s32[64]{0:T(128)S(1)} %multiply_add_fusion), kind=kOutput, calls=%fused_computation.24 | convolution fusion | flops 33824768 | bytes 557312 | tf_op jit(solution)/shard_map/dot_general | solution.py:51
  10.3 7.4 %all-to-all-start = ((bf16[16,8,2048]{2,1,0:T(8,128)(2,1)}), bf16[16,8,2048]{2,1,0:T(8,128)(2,1)}, u32[]{:S(2)}, u32[]{:S(2)}) async-start(bf16[16,8,2048]{2,1,0:T(8,128)(2,1)} %fusion.24), calls=%async_computation | async-start | bytes 1048576 | tf_op jit(solution)/shard_map/all_to_all | solution.py:60
  17.7 0.8 mul.60
  18.5 0.8 convert_element_type.77
  19.3 1.1 fusion.25
  20.4 11.8 %all-to-all-done = bf16[16,8,2048]{2,1,0:T(8,128)(2,1)} async-done(((bf16[16,8,2048]{2,1,0:T(8,128)(2,1)}), bf16[16,8,2048]{2,1,0:T(8,128)(2,1)}, u32[]{:S(2)}, u32[]{:S(2)}) %all-to-all-start) | async-done | bytes 524320 | tf_op jit(solution)/shard_map/all_to_all | solution.py:60
  32.2 4.2 %all-to-all-start.2 = ((bf16[16,8,2048]{2,1,0:T(8,128)(2,1)}), bf16[16,8,2048]{2,1,0:T(8,128)(2,1)}, u32[]{:S(2)}, u32[]{:S(2)}) async-start(bf16[16,8,2048]{2,1,0:T(8,128)(2,1)} %fusion.25), calls=%async_computation.2 | async-start | bytes 1048576 | tf_op jit(solution)/shard_map/all_to_all | solution.py:61
  36.5 0.0 all-reduce.3.cloned.1.call-start
  36.6 0.0 copy-start.1
  36.6 3.5 %fusion.35 = bf16[128,768]{1,0:T(8,128)(2,1)} fusion(bf16[1,2048,768]{2,1,0:T(8,128)(2,1)} %param.11, bf16[16,8,2048]{2,1,0:T(8,128)(2,1)} %all-to-all-done), kind=kOutput, calls=%fused_computation.29 | convolution fusion | flops 402751488 | bytes 3866624 | tf_op jit(solution)/shard_map/dot_general | solution.py:69
  40.0 2.3 %fusion.32 = bf16[128,768]{1,0:T(8,128)(2,1)} fusion(bf16[1,2048,768]{2,1,0:T(8,128)(2,1)S(1)} %copy-done.1, bf16[16,8,2048]{2,1,0:T(8,128)(2,1)} %all-to-all-done), kind=kOutput, calls=%fused_computation.28 | convolution fusion | flops 402751488 | bytes 3866624 | tf_op jit(solution)/shard_map/dot_general | solution.py:68
  42.3 8.6 %all-to-all-done.2 = bf16[16,8,2048]{2,1,0:T(8,128)(2,1)} async-done(((bf16[16,8,2048]{2,1,0:T(8,128)(2,1)}), bf16[16,8,2048]{2,1,0:T(8,128)(2,1)}, u32[]{:S(2)}, u32[]{:S(2)}) %all-to-all-start.2) | async-done | bytes 524320 | tf_op jit(solution)/shard_map/all_to_all | solution.py:61
  51.0 2.9 %fusion.38 = bf16[128,768]{1,0:T(8,128)(2,1)} fusion(bf16[1,768,2048]{2,1,0:T(8,128)(2,1)S(1)} %copy-done, bf16[16,8,2048]{2,1,0:T(8,128)(2,1)} %all-to-all-done.2), kind=kOutput, calls=%fused_computation.30 | convolution fusion | flops 402751488 | bytes 3866624 | tf_op jit(solution)/shard_map/dot_general | solution.py:34
  53.9 0.0 all-reduce.3.cloned.1.call-update
  53.9 30.0 %all-reduce.3.cloned.1.call-done = (bf16[128,768]{1,0:T(8,128)(2,1)}, bf16[128,768]{1,0:T(8,128)(2,1)}, bf16[128,768]{1,0:T(8,128)(2,1)}) async-done(((bf16[128,768]{1,0:T(8,128)(2,1)}, bf16[128,768]{1,0:T(8,128)(2,1)}, bf16[128,768]{1,0:T(8,128)(2,1)}), (bf16[128,768]{1,0:T(8,128)(2,1)}, bf16[128,768]{1,0:T(8,128)(2,1)}, bf16[128,768]{1,0:T(8,128)(2,1)})) %all-reduce.3.cloned.1.call-update) | async-done | bytes 589840 | tf_op jit(solution)/shard_map/psum | solution.py:72
  83.9 2.5 %fusion.26 = bf16[16,8,2048]{2,1,0:T(8,128)(2,1)} fusion(bf16[1,768,2048]{2,1,0:T(8,128)(2,1)S(1)} %copy-done, bf16[128,768]{1,0:T(8,128)(2,1)} %get-tuple-element.5, bf16[128,768]{1,0:T(8,128)(2,1)} %get-tuple-element.6), kind=kOutput, calls=%fused_computation.26 | convolution fusion | flops 403701760 | bytes 4063232 | tf_op jit(solution)/shard_map/dot_general | solution.py:75
  86.3 5.8 %all-to-all-start.1 = ((bf16[16,8,2048]{2,1,0:T(8,128)(2,1)}), bf16[16,8,2048]{2,1,0:T(8,128)(2,1)}, u32[]{:S(2)}, u32[]{:S(2)}) async-start(bf16[16,8,2048]{2,1,0:T(8,128)(2,1)} %fusion.26), calls=%async_computation.1 | async-start | bytes 1048576 | tf_op jit(solution)/shard_map/all_to_all | solution.py:90
  92.2 3.3 %fusion.4 = f32[128,2048]{1,0:T(8,128)S(1)} fusion(bf16[1,2048,768]{2,1,0:T(8,128)(2,1)} %param.11, bf16[128,768]{1,0:T(8,128)(2,1)} %get-tuple-element.7, bf16[128,768]{1,0:T(8,128)(2,1)S(1)} %copy-done.3), kind=kOutput, calls=%fused_computation.7 | convolution fusion | flops 403439616 | bytes 4587520 | tf_op jit(solution)/shard_map/dot_general | solution.py:34
  95.5 2.0 %fusion.29 = bf16[16,8,2048]{2,1,0:T(8,128)(2,1)} fusion(f32[128,2048]{1,0:T(8,128)S(1)} %fusion.4, bf16[1,2048,768]{2,1,0:T(8,128)(2,1)S(1)} %copy-done.2, bf16[128,768]{1,0:T(8,128)(2,1)S(1)} %copy-done.4, bf16[128,768]{1,0:T(8,128)(2,1)S(1)} %copy-done.5, bf16[128,768]{1,0:T(8,128)(2,1)S(1)} %copy-done.3), kind=kOutput, calls=%fused_computation.27 | convolution fusion | flops 404455424 | bytes 5308416 | tf_op jit(solution)/shard_map/dot_general | solution.py:34
  97.4 9.2 %all-to-all-done.1 = bf16[16,8,2048]{2,1,0:T(8,128)(2,1)} async-done(((bf16[16,8,2048]{2,1,0:T(8,128)(2,1)}), bf16[16,8,2048]{2,1,0:T(8,128)(2,1)}, u32[]{:S(2)}, u32[]{:S(2)}) %all-to-all-start.1) | async-done | bytes 524320 | tf_op jit(solution)/shard_map/all_to_all | solution.py:90
  106.7 4.2 %all-to-all-start.3 = ((bf16[16,8,2048]{2,1,0:T(8,128)(2,1)}), bf16[16,8,2048]{2,1,0:T(8,128)(2,1)}, u32[]{:S(2)}, u32[]{:S(2)}) async-start(bf16[16,8,2048]{2,1,0:T(8,128)(2,1)} %fusion.29), calls=%async_computation.3 | async-start | bytes 1048576 | tf_op jit(solution)/shard_map/all_to_all | solution.py:91
  110.9 3.8 %fusion.14 = bf16[1,768,2048]{2,1,0:T(8,128)(2,1)} fusion(bf16[16,8,2048]{2,1,0:T(8,128)(2,1)} %all-to-all-done.2, bf16[128,768]{1,0:T(8,128)(2,1)S(1)} %copy-done.4, bf16[128,768]{1,0:T(8,128)(2,1)S(1)} %copy-done.3), kind=kOutput, calls=%fused_computation.17 | convolution fusion | flops 405012480 | bytes 4063232 | tf_op jit(solution)/shard_map/dot_general | solution.py:28
  114.7 3.7 %fusion.13 = bf16[1,2048,768]{2,1,0:T(8,128)(2,1)} fusion(bf16[16,8,2048]{2,1,0:T(8,128)(2,1)} %all-to-all-done, bf16[128,768]{1,0:T(8,128)(2,1)S(1)} %copy-done.6, bf16[128,768]{1,0:T(8,128)(2,1)S(1)} %copy-done.3), kind=kOutput, calls=%fused_computation.16 | convolution fusion | flops 405012480 | bytes 4063232 | tf_op jit(solution)/shard_map/dot_general | solution.py:28
  118.5 3.8 %fusion.12 = bf16[1,2048,768]{2,1,0:T(8,128)(2,1)} fusion(bf16[16,8,2048]{2,1,0:T(8,128)(2,1)} %all-to-all-done, bf16[128,768]{1,0:T(8,128)(2,1)S(1)} %copy-done.4, bf16[128,768]{1,0:T(8,128)(2,1)S(1)} %copy-done.6, bf16[128,768]{1,0:T(8,128)(2,1)S(1)} %copy-done.3), kind=kOutput, calls=%fused_computation.15 | convolution fusion | flops 405504000 | bytes 4259840 | tf_op jit(solution)/shard_map/dot_general | solution.py:28
  122.2 2.0 %fusion.41 = bf16[8,2048]{1,0:T(8,128)(2,1)} fusion(bf16[16,8,2048]{2,1,0:T(8,128)(2,1)} %all-to-all-done.1, f32[8,8]{1,0:T(8,128)S(1)} %copy-done.7, s32[64]{0:T(128)S(1)} %multiply_add_fusion), kind=kOutput, calls=%fused_computation.32 | convolution fusion | flops 33808384 | bytes 557568 | tf_op jit(solution)/shard_map/dot_general | solution.py:28
  124.3 1.1 all-to-all-done.3
  125.4 2.0 %convolution_reduce_fusion = bf16[8,2048]{1,0:T(8,128)(2,1)} fusion(bf16[16,8,2048]{2,1,0:T(8,128)(2,1)} %all-to-all-done.3, s32[64]{0:T(128)S(1)} %multiply_add_fusion), kind=kOutput, calls=%fused_computation.31 | convolution fusion | flops 33677312 | bytes 557312 | tf_op jit(solution)/shard_map/dot_general | solution.py:28
  (15 shorter events, 0.0 us)
Async XLA Ops:
  7.2 43.8 %copy-start = (bf16[1,768,2048]{2,1,0:T(8,128)(2,1)S(1)}, bf16[1,768,2048]{2,1,0:T(8,128)(2,1)}, u32[]{:S(2)}) copy-start(bf16[1,768,2048]{2,1,0:T(8,128)(2,1)} %param.12) | copy-start | bytes 9437188
  10.3 21.9 %all-to-all-start = ((bf16[16,8,2048]{2,1,0:T(8,128)(2,1)}), bf16[16,8,2048]{2,1,0:T(8,128)(2,1)}, u32[]{:S(2)}, u32[]{:S(2)}) async-start(bf16[16,8,2048]{2,1,0:T(8,128)(2,1)} %fusion.24), calls=%async_computation | async-start | bytes 1048576 | tf_op jit(solution)/shard_map/all_to_all | solution.py:60
  32.2 18.7 %all-to-all-start.2 = ((bf16[16,8,2048]{2,1,0:T(8,128)(2,1)}), bf16[16,8,2048]{2,1,0:T(8,128)(2,1)}, u32[]{:S(2)}, u32[]{:S(2)}) async-start(bf16[16,8,2048]{2,1,0:T(8,128)(2,1)} %fusion.25), calls=%async_computation.2 | async-start | bytes 1048576 | tf_op jit(solution)/shard_map/all_to_all | solution.py:61
  36.5 47.3 %all-reduce.3.cloned.1.call-start = ((), (), s32[]{:S(2)}) async-start(), calls=%async_computation.4 | async-start | bytes 1179648 | tf_op jit(solution)/shard_map/psum | solution.py:72
  36.6 3.5 %copy-start.1 = (bf16[1,2048,768]{2,1,0:T(8,128)(2,1)S(1)}, bf16[1,2048,768]{2,1,0:T(8,128)(2,1)}, u32[]{:S(2)}) copy-start(bf16[1,2048,768]{2,1,0:T(8,128)(2,1)} %param.10) | copy-start | bytes 9437188
  83.8 8.3 %copy-start.3 = (bf16[128,768]{1,0:T(8,128)(2,1)S(1)}, bf16[128,768]{1,0:T(8,128)(2,1)}, u32[]{:S(2)}) copy-start(bf16[128,768]{1,0:T(8,128)(2,1)} %get-tuple-element.6) | copy-start | bytes 589828
  86.3 9.1 %copy-start.4 = (bf16[128,768]{1,0:T(8,128)(2,1)S(1)}, bf16[128,768]{1,0:T(8,128)(2,1)}, u32[]{:S(2)}) copy-start(bf16[128,768]{1,0:T(8,128)(2,1)} %get-tuple-element.5) | copy-start | bytes 589828
  86.3 20.3 %all-to-all-start.1 = ((bf16[16,8,2048]{2,1,0:T(8,128)(2,1)}), bf16[16,8,2048]{2,1,0:T(8,128)(2,1)}, u32[]{:S(2)}, u32[]{:S(2)}) async-start(bf16[16,8,2048]{2,1,0:T(8,128)(2,1)} %fusion.26), calls=%async_computation.1 | async-start | bytes 1048576 | tf_op jit(solution)/shard_map/all_to_all | solution.py:90
  92.1 3.3 %copy-start.2 = (bf16[1,2048,768]{2,1,0:T(8,128)(2,1)S(1)}, bf16[1,2048,768]{2,1,0:T(8,128)(2,1)}, u32[]{:S(2)}) copy-start(bf16[1,2048,768]{2,1,0:T(8,128)(2,1)} %param.10) | copy-start | bytes 9437188
  92.2 3.3 %copy-start.5 = (bf16[128,768]{1,0:T(8,128)(2,1)S(1)}, bf16[128,768]{1,0:T(8,128)(2,1)}, u32[]{:S(2)}) copy-start(bf16[128,768]{1,0:T(8,128)(2,1)} %get-tuple-element.7) | copy-start | bytes 589828
  106.7 18.7 %all-to-all-start.3 = ((bf16[16,8,2048]{2,1,0:T(8,128)(2,1)}), bf16[16,8,2048]{2,1,0:T(8,128)(2,1)}, u32[]{:S(2)}, u32[]{:S(2)}) async-start(bf16[16,8,2048]{2,1,0:T(8,128)(2,1)} %fusion.29), calls=%async_computation.3 | async-start | bytes 1048576 | tf_op jit(solution)/shard_map/all_to_all | solution.py:91
  110.9 3.8 %copy-start.6 = (bf16[128,768]{1,0:T(8,128)(2,1)S(1)}, bf16[128,768]{1,0:T(8,128)(2,1)}, u32[]{:S(2)}) copy-start(bf16[128,768]{1,0:T(8,128)(2,1)} %get-tuple-element.7) | copy-start | bytes 589828
  118.5 3.8 %copy-start.7 = (f32[8,8]{1,0:T(8,128)S(1)}, f32[8,8]{1,0:T(8,128)}, u32[]{:S(2)}) copy-start(f32[8,8]{1,0:T(8,128)} %param.9) | copy-start | bytes 772
Sparse Core Ops, SparseCore 0:
  54.0 29.7 all-reduce.2
where the time goes:
time: 135 us; the launch traced here: 134 us
  waiting for transfers between devices  60.8 us (45%)
  matrix products  34.7 us (26%)
  starting transfers between devices  21.7 us (16%)
  between operations  14.2 us (11%)
  local copies, waits for them, and re-layouts  1.72 us (1%)
    psum x1, waiting for transfers between devices, local(): lax.psum(up_part.astype(jnp.bfloat16), 'dp').astype(jnp.float32)  30 us
    dot_general x5, matrix products, contract_rows(): lax.dot_general(left, right, (((0,), (0,)), ((), ())), preferred_element_...  15.3 us
    all_to_all x1, waiting for transfers between devices, local(): lax.all_to_all(dispatch_token_rows, 'expert', split_axis=0, concat_axis=0...  11.8 us
    all_to_all x1, waiting for transfers between devices, local(): lax.all_to_all(out_blocks, 'expert', split_axis=0, concat_axis=0, tiled=T...  9.22 us
    all_to_all x1, waiting for transfers between devices, local(): lax.all_to_all(dispatch_gradients, 'expert', split_axis=0, concat_axis=0,...  8.64 us
    dot_general x3, matrix products, contract_cols(): lax.dot_general(left, right, (((1,), (1,)), ((), ())), preferred_element_...  8.13 us
    all_to_all x1, starting transfers between devices, local(): lax.all_to_all(dispatch_token_rows, 'expert', split_axis=0, concat_axis=0...  7.41 us
    all_to_all x1, starting transfers between devices, local(): lax.all_to_all(out_blocks, 'expert', split_axis=0, concat_axis=0, tiled=T...  5.8 us
  transfers between devices with their start and end apart: 5, of which 5 were waited for; matrix products, arithmetic and copies ran while one was open for 20% of the time, Pallas kernels for 0%

commit v1 on v0

--- a/solution.py
+++ b/solution.py
@@ -1,7 +1,14 @@
+import functools
+
 import jax
 import jax.numpy as jnp
 from jax import lax
+from jax.experimental import pallas as pl
+from jax.experimental.pallas import tpu as pltpu
 from jax.sharding import PartitionSpec as P
+
+MESH = pl.DeviceIdType.MESH
+LANES = 128
 
 
 def slot_table(id_block, experts, capacity):
@@ -36,7 +43,7 @@
     )
 
 
-def local(tokens, expert_ids, route_weights, w_gate, w_up, w_down, grad_out):
+def general(tokens, expert_ids, route_weights, w_gate, w_up, w_down, grad_out):
     tok_rows = tokens.shape[0]
     slices = tokens.shape[1]
     top_count = expert_ids.shape[1]
@@ -101,6 +108,356 @@
     return (layer_out, input_grad, gate_weight[None], up_weight[None], down_grad[None])
 
 
+def partner(index, step):
+    bit = 1
+    while bit <= step:
+        if step & bit:
+            index = index + bit - 2 * bit * ((index // bit) % 2)
+        bit *= 2
+    return index
+
+
+def exchange_kernel(
+    planes,
+    tok_ref, grad_ref, id_ref, weight_ref, gate_hbm, up_hbm, down_hbm,
+    x_ref, eg_ref, hidden_ref, gg_ref, ug_ref, sum_ref,
+    w_gate, w_up, w_down, load_sem,
+    msg, scale, part, other, back, back_sib, mid, mid_x, last, last_z,
+    z_send, z_recv, x_send, x_recv, s_send, s_recv, y_send, y_recv,
+    r1_send, r1_recv, r2_send, r2_recv, r3_send, r3_recv,
+):
+    rows, wide = tok_ref.shape
+    ff = w_gate.shape[1]
+    top = id_ref.shape[1]
+    chunk = 4 * rows
+    me = lax.axis_index("expert")
+    core = me % 2
+    side = (me // 2) % 2
+    plane = me // 4
+    pair = {"dp": 1 - lax.axis_index("dp")}
+    sibling = {"expert": plane * 4 + side * 2 + (1 - core)}
+    across = {"expert": plane * 4 + (1 - side) * 2 + core}
+
+    def in_plane(step):
+        return {"expert": partner(plane, step) * 4 + side * 2 + core}
+
+    loads = []
+    for i, (source, target) in enumerate(
+        ((gate_hbm, w_gate), (up_hbm, w_up), (down_hbm, w_down))
+    ):
+        load = pltpu.make_async_copy(source.at[0], target, load_sem.at[i])
+        load.start()
+        loads.append(load)
+
+    peers = [sibling, across, pair] + [in_plane(step) for step in range(1, planes)]
+    barrier = pltpu.get_barrier_semaphore()
+    for peer in peers:
+        pl.semaphore_signal(barrier, inc=1, device_id=peer, device_id_type=MESH)
+
+    lane = lax.broadcasted_iota(jnp.int32, (rows, LANES), 1)
+    dense = jnp.zeros((rows, LANES), jnp.float32)
+    chosen = jnp.zeros((rows, LANES), jnp.float32)
+    for k in range(top):
+        hit = id_ref[:, k:k + 1] == lane
+        dense = dense + jnp.where(hit, weight_ref[:, k:k + 1], 0.0)
+        chosen = chosen + jnp.where(hit, 1.0, 0.0)
+    high = dense.astype(jnp.bfloat16).astype(jnp.float32)
+    middle = (dense - high).astype(jnp.bfloat16).astype(jnp.float32)
+    low = dense - high - middle
+    both = jnp.concatenate(
+        [tok_ref[...].astype(jnp.float32), grad_ref[...].astype(jnp.float32)], axis=0
+    )
+    extra_a = jnp.concatenate([high, low], axis=0)
+    extra_b = jnp.concatenate([middle, chosen], axis=0)
+    msg[0, side, core, :, :wide] = both.astype(jnp.bfloat16)
+    msg[0, side, core, :, wide:wide + LANES] = extra_a.astype(jnp.bfloat16)
+    msg[0, side, core, :, wide + LANES:] = extra_b.astype(jnp.bfloat16)
+
+    pl.semaphore_wait(barrier, len(peers))
+
+    sends = []
+
+    def send(source, target, send_sem, recv_sem, device):
+        copy = pltpu.make_async_remote_copy(
+            src_ref=source, dst_ref=target, send_sem=send_sem, recv_sem=recv_sem,
+            device_id=device, device_id_type=MESH,
+        )
+        copy.start()
+        sends.append(copy)
+
+    def arrived(target, send_sem, recv_sem, device):
+        pltpu.make_async_remote_copy(
+            src_ref=target, dst_ref=target, send_sem=send_sem, recv_sem=recv_sem,
+            device_id=device, device_id_type=MESH,
+        ).wait_recv()
+
+    def spread(k):
+        own = msg.at[k, side, core]
+        if k > 0:
+            arrived(own, z_send.at[k], z_recv.at[k], in_plane(k))
+        send(own, own, x_send.at[k], x_recv.at[k], across)
+        send(own, own, s_send.at[k, 0], s_recv.at[k, 0], sibling)
+
+    def relay(k):
+        far = msg.at[k, 1 - side, core]
+        arrived(far, x_send.at[k], x_recv.at[k], across)
+        send(far, far, s_send.at[k, 1], s_recv.at[k, 1], sibling)
+
+    def gather_end(k):
+        arrived(msg.at[k, side, 1 - core], s_send.at[k, 0], s_recv.at[k, 0], sibling)
+        arrived(msg.at[k, 1 - side, 1 - core], s_send.at[k, 1], s_recv.at[k, 1], sibling)
+
+    def first_half(k):
+        mine = lax.broadcasted_iota(jnp.int32, (rows, LANES), 1) == me
+        at = k * chunk
+        for s in range(2):
+            ins, grads = [], []
+            for c in range(2):
+                extra = msg[k, s, c, :, wide:].astype(jnp.float32)
+                dense_w = extra[:rows, :LANES] + extra[:rows, LANES:] + extra[rows:, :LANES]
+                weight = jnp.sum(jnp.where(mine, dense_w, 0.0), axis=1, keepdims=True)
+                mask = jnp.sum(jnp.where(mine, extra[rows:, LANES:], 0.0), axis=1, keepdims=True)
+                body = msg[k, s, c, :, :wide].astype(jnp.float32)
+                ins.append(body[:rows] * mask)
+                grads.append(body[rows:] * weight)
+                j = 2 * s + c
+                scale[k, j * rows:(j + 1) * rows, :] = jnp.broadcast_to(weight, (rows, LANES))
+            here = slice(at + 2 * s * rows, at + 2 * (s + 1) * rows)
+            x_ref[here, :] = jnp.concatenate(ins, axis=0).astype(jnp.bfloat16)
+            eg_ref[here, :] = jnp.concatenate(grads, axis=0).astype(jnp.bfloat16)
+
+        tile = min(256, ff)
+        span = slice(at, at + chunk)
+
+        def give(i):
+            send(part.at[k, i], other.at[k, i], y_send.at[k, i], y_recv.at[k, i], pair)
+
+        for i, matrix in enumerate((w_gate, w_up)):
+            if k == 0:
+                loads[i].wait()
+
+            @pl.loop(0, ff // tile)
+            def _(n):
+                cols = pl.ds(pl.multiple_of(n * tile, tile), tile)
+                part[k, i, :, cols] = jnp.dot(
+                    x_ref[span, :], matrix[:, cols], preferred_element_type=jnp.float32
+                ).astype(jnp.bfloat16)
+
+            give(i)
+        if k == 0:
+            loads[2].wait()
+
+        @pl.loop(0, ff // tile)
+        def _(n):
+            cols = pl.ds(pl.multiple_of(n * tile, tile), tile)
+            part[k, 2, :, cols] = contract_cols(eg_ref[span, :], w_down[cols, :]).astype(
+                jnp.bfloat16
+            )
+
+        give(2)
+
+    def second_half(k):
+        span = slice(k * chunk, (k + 1) * chunk)
+        for i in range(3):
+            arrived(other.at[k, i], y_send.at[k, i], y_recv.at[k, i], pair)
+        gate, up_value, hidden_grad = [
+            part[k, i].astype(jnp.float32) + other[k, i].astype(jnp.float32) for i in range(3)
+        ]
+        sig = jax.nn.sigmoid(gate)
+        silu = gate * sig
+        hidden_ref[span, :] = (silu * up_value).astype(jnp.bfloat16)
+        gg_ref[span, :] = (
+            hidden_grad * up_value * sig * (1.0 + gate * (1.0 - sig))
+        ).astype(jnp.bfloat16)
+        ug_ref[span, :] = (hidden_grad * silu).astype(jnp.bfloat16)
+        tile = min(512, wide)
+
+        @pl.loop(0, wide // tile)
+        def _(n):
+            cols = pl.ds(pl.multiple_of(n * tile, tile), tile)
+            out = jnp.dot(
+                hidden_ref[span, :], w_down[:, cols], preferred_element_type=jnp.float32
+            ) * scale[k, :, 0:1]
+            back_in = contract_cols(gg_ref[span, :], w_gate[cols, :]) + contract_cols(
+                ug_ref[span, :], w_up[cols, :]
+            )
+            for s in range(2):
+                for c in range(2):
+                    block = slice((2 * s + c) * rows, (2 * s + c + 1) * rows)
+                    back[k, c, s, :, cols] = jnp.concatenate(
+                        [out[block], back_in[block]], axis=0
+                    ).astype(jnp.bfloat16)
+
+        send(back.at[k, 1 - core], back_sib.at[k], r1_send.at[k], r1_recv.at[k], sibling)
+
+    def sum_core(k):
+        arrived(back_sib.at[k], r1_send.at[k], r1_recv.at[k], sibling)
+        mid[k] = (
+            back[k, core].astype(jnp.float32) + back_sib[k].astype(jnp.float32)
+        ).astype(jnp.bfloat16)
+        send(mid.at[k, 1 - side], mid_x.at[k], r2_send.at[k], r2_recv.at[k], across)
+
+    def sum_side(k):
+        arrived(mid_x.at[k], r2_send.at[k], r2_recv.at[k], across)
+        last[k] = (
+            mid[k, side].astype(jnp.float32) + mid_x[k].astype(jnp.float32)
+        ).astype(jnp.bfloat16)
+        if k > 0:
+            send(last.at[k], last_z.at[k], r3_send.at[k], r3_recv.at[k], in_plane(k))
+
+    own = msg.at[0, side, core]
+    spread(0)
+    for k in range(1, planes):
+        send(own, msg.at[k, side, core], z_send.at[k], z_recv.at[k], in_plane(k))
+
+    ahead = min(2, planes - 1)
+    for k in range(planes + ahead):
+        if k < planes:
+            relay(k)
+            if k + 1 < planes:
+                spread(k + 1)
+            gather_end(k)
+            first_half(k)
+        done = k - ahead
+        if done >= 0:
+            second_half(done)
+            if done >= 1:
+                sum_core(done - 1)
+            if done >= 2:
+                sum_side(done - 2)
+    if planes >= 2:
+        sum_side(planes - 2)
+    sum_core(planes - 1)
+    sum_side(planes - 1)
+
+    total = last[0].astype(jnp.float32)
+    for k in range(1, planes):
+        arrived(last_z.at[k], r3_send.at[k], r3_recv.at[k], in_plane(k))
+        total = total + last_z[k].astype(jnp.float32)
+    sum_ref[...] = total.astype(jnp.bfloat16)
+    for copy in sends:
+        copy.wait_send()
+
+
+def exchange(tokens, expert_ids, route_weights, w_gate, w_up, w_down, grad_out):
+    rows, wide = tokens.shape
+    ff = w_gate.shape[2]
+    experts = lax.axis_size("expert")
+    planes = experts // 4
+    total = experts * rows
+    chunk = 4 * rows
+    bf16 = jnp.bfloat16
+    vmem = pl.BlockSpec(memory_space=pltpu.VMEM)
+    hbm = pl.BlockSpec(memory_space=pl.ANY)
+    dma = pltpu.SemaphoreType.DMA
+    return pl.pallas_call(
+        functools.partial(exchange_kernel, planes),
+        out_shape=(
+            jax.ShapeDtypeStruct((total, wide), bf16),
+            jax.ShapeDtypeStruct((total, wide), bf16),
+            jax.ShapeDtypeStruct((total, ff), bf16),
+            jax.ShapeDtypeStruct((total, ff), bf16),
+            jax.ShapeDtypeStruct((total, ff), bf16),
+            jax.ShapeDtypeStruct((2 * rows, wide), bf16),
+        ),
+        in_specs=[vmem] * 4 + [hbm] * 3,
+        out_specs=(vmem,) * 6,
+        scratch_shapes=[
+            pltpu.VMEM((wide, ff), bf16),
+            pltpu.VMEM((wide, ff), bf16),
+            pltpu.VMEM((ff, wide), bf16),
+            dma((3,)),
+            pltpu.VMEM((planes, 2, 2, 2 * rows, wide + 2 * LANES), bf16),
+            pltpu.VMEM((planes, chunk, LANES), jnp.float32),
+            pltpu.VMEM((planes, 3, chunk, ff), bf16),
+            pltpu.VMEM((planes, 3, chunk, ff), bf16),
+            pltpu.VMEM((planes, 2, 2, 2 * rows, wide), bf16),
+            pltpu.VMEM((planes, 2, 2 * rows, wide), bf16),
+            pltpu.VMEM((planes, 2, 2 * rows, wide), bf16),
+            pltpu.VMEM((planes, 2 * rows, wide), bf16),
+            pltpu.VMEM((planes, 2 * rows, wide), bf16),
+            pltpu.VMEM((planes, 2 * rows, wide), bf16),
+            dma((planes,)), dma((planes,)),
+            dma((planes,)), dma((planes,)),
+            dma((planes, 2)), dma((planes, 2)),
+            dma((planes, 3)), dma((planes, 3)),
+            dma((planes,)), dma((planes,)),
+            dma((planes,)), dma((planes,)),
+            dma((planes,)), dma((planes,)),
+        ],
+        compiler_params=pltpu.CompilerParams(
+            collective_id=0, has_side_effects=True, vmem_limit_bytes=48 * 1024 * 1024
+        ),
+        name="exchange",
+    )(tokens, grad_out, expert_ids, route_weights, w_gate, w_up, w_down)
+
+
+def weights_kernel(x_ref, eg_ref, hidden_ref, gg_ref, ug_ref, sum_ref,
+                   out_ref, in_ref, gate_ref, up_ref, down_ref):
+    rows = out_ref.shape[0]
+    gate_ref[0] = contract_rows(x_ref[...], gg_ref[...]).astype(jnp.bfloat16)
+    up_ref[0] = contract_rows(x_ref[...], ug_ref[...]).astype(jnp.bfloat16)
+    down_ref[0] = contract_rows(hidden_ref[...], eg_ref[...]).astype(jnp.bfloat16)
+
+    @pl.when(pl.program_id(0) == 0)
+    def _():
+        both = sum_ref[...].astype(jnp.float32)
+        out_ref[...] = both[:rows].astype(jnp.bfloat16)
+        in_ref[...] = both[rows:].astype(jnp.bfloat16)
+
+
+def weight_grads(x, eg, hidden, gg, ug, sums):
+    total, wide = x.shape
+    ff = hidden.shape[1]
+    rows = sums.shape[0] // 2
+    tile = min(256, wide)
+    bf16 = jnp.bfloat16
+
+    def whole(shape):
+        return pl.BlockSpec(shape, lambda n: (0,) * len(shape))
+
+    cols = pl.BlockSpec((total, tile), lambda n: (0, n))
+    return pl.pallas_call(
+        weights_kernel,
+        grid=(wide // tile,),
+        out_shape=(
+            jax.ShapeDtypeStruct((rows, wide), bf16),
+            jax.ShapeDtypeStruct((rows, wide), bf16),
+            jax.ShapeDtypeStruct((1, wide, ff), bf16),
+            jax.ShapeDtypeStruct((1, wide, ff), bf16),
+            jax.ShapeDtypeStruct((1, ff, wide), bf16),
+        ),
+        in_specs=[cols, cols] + [whole((total, ff))] * 3 + [whole((2 * rows, wide))],
+        out_specs=(
+            whole((rows, wide)),
+            whole((rows, wide)),
+            pl.BlockSpec((1, tile, ff), lambda n: (0, n, 0)),
+            pl.BlockSpec((1, tile, ff), lambda n: (0, n, 0)),
+            pl.BlockSpec((1, ff, tile), lambda n: (0, 0, n)),
+        ),
+        compiler_params=pltpu.CompilerParams(vmem_limit_bytes=32 * 1024 * 1024),
+        name="weight_grads",
+    )(x, eg, hidden, gg, ug, sums)
+
+
+def local(tokens, expert_ids, route_weights, w_gate, w_up, w_down, grad_out):
+    experts = lax.axis_size("expert")
+    planes = experts // 4
+    fits = (
+        lax.axis_size("dp") == 2
+        and experts % 4 == 0
+        and planes & (planes - 1) == 0
+        and planes <= 4
+        and experts <= LANES
+        and tokens.shape[0] % 8 == 0
+    )
+    if not fits:
+        return general(tokens, expert_ids, route_weights, w_gate, w_up, w_down, grad_out)
+    return weight_grads(
+        *exchange(tokens, expert_ids, route_weights, w_gate, w_up, w_down, grad_out)
+    )
+
+
 def solution(mesh):
     return jax.shard_map(
         local,

time: 135 us -> 61.2 us (0.45)
  waiting for transfers between devices: 60.8 us -> 0 us
  Pallas kernels: 0 us -> 55.4 us
  matrix products: 34.7 us -> 0 us
  starting transfers between devices: 21.7 us -> 0 us
  between operations: 14.2 us -> 0.65 us
  local copies, waits for them, and re-layouts: 1.72 us -> 4.77 us
    pallas_call x0 -> x2, Pallas kernels: none -> 55.4 us  [the longest x1 48.8 us: exchange(): pl.pallas_call(functools.partial(exchange_kernel, planes), out_shape=(jax...]
    dot_general x13 -> x0, matrix products: 34.7 us -> none  [the longest x5 15.3 us: contract_rows(): lax.dot_general(left, right, (((0,), (0,)), ((), ())), preferred_element_...]
    all_to_all x4 -> x0, waiting for transfers between devices: 30.8 us -> none  [the longest x1 11.8 us: local(): lax.all_to_all(dispatch_token_rows, 'expert', split_axis=0, concat_axis=0...]
    psum x1 -> x0, waiting for transfers between devices: 30 us -> none  [local(): lax.psum(up_part.astype(jnp.bfloat16), 'dp').astype(jnp.float32)]
    all_to_all x4 -> x0, starting transfers between devices: 21.7 us -> none  [the longest x1 7.41 us: local(): lax.all_to_all(dispatch_token_rows, 'expert', split_axis=0, concat_axis=0...]
    unnamed x16 -> x10, local copies, waits for them, and re-layouts: 0.04 us -> 4.77 us
  transfers between devices with their start and end apart: 5 -> 0, of which waited for: 5 -> 0; matrix products, arithmetic and copies ran while one was open for 20% -> 0% of each run, Pallas kernels for 0% -> 0%
where the time goes in v1:
time: 61.2 us; the launch traced here: 60.9 us
  Pallas kernels  55.4 us (91%)
  local copies, waits for them, and re-layouts  4.77 us (8%)
  between operations  0.65 us (1%)
    pallas_call x1, Pallas kernels, exchange(): pl.pallas_call(functools.partial(exchange_kernel, planes), out_shape=(jax...  48.8 us
    pallas_call x1, Pallas kernels, weight_grads(): pl.pallas_call(weights_kernel, grid=(wide // tile,), out_shape=(jax.Shape...  6.65 us
    unnamed x10, local copies, waits for them, and re-layouts  4.77 us

profile of v1, /device:TPU:0, one launch (start us, length us, event | category | flops | bytes accessed | tf_op | source)
XLA Modules:
  0.0 60.9 jit_solution(13403407986128704326)
XLA Ops:
  0.6 0.0 copy-start
  0.6 1.9 %copy-done = bf16[1,2048,768]{2,1,0:T(8,128)(2,1)S(1)} copy-done((bf16[1,2048,768]{2,1,0:T(8,128)(2,1)S(1)}, bf16[1,2048,768]{2,1,0:T(8,128)(2,1)}, u32[]{:S(2)}) %copy-start) | copy-done | bytes 3145752
  2.5 0.0 copy-start.1
  2.5 0.8 %copy-done.1 = bf16[8,2048]{1,0:T(8,128)(2,1)S(1)} copy-done((bf16[8,2048]{1,0:T(8,128)(2,1)S(1)}, bf16[8,2048]{1,0:T(8,128)(2,1)}, u32[]{:S(2)}) %copy-start.1) | copy-done | bytes 32792
  3.3 0.0 copy-start.2
  3.3 0.8 %copy-done.2 = bf16[8,2048]{1,0:T(8,128)(2,1)S(1)} copy-done((bf16[8,2048]{1,0:T(8,128)(2,1)S(1)}, bf16[8,2048]{1,0:T(8,128)(2,1)}, u32[]{:S(2)}) %copy-start.2) | copy-done | bytes 32792
  4.0 0.0 copy-start.3
  4.0 0.7 %copy-done.3 = s32[8,8]{1,0:T(8,128)S(1)} copy-done((s32[8,8]{1,0:T(8,128)S(1)}, s32[8,8]{1,0:T(8,128)}, u32[]{:S(2)}) %copy-start.3) | copy-done | bytes 280
  4.7 0.0 copy-start.4
  4.7 0.7 %copy-done.4 = f32[8,8]{1,0:T(8,128)S(1)} copy-done((f32[8,8]{1,0:T(8,128)S(1)}, f32[8,8]{1,0:T(8,128)}, u32[]{:S(2)}) %copy-start.4) | copy-done | bytes 280
  5.4 48.8 %exchange.1 = (bf16[128,2048]{1,0:T(8,128)(2,1)S(1)}, bf16[128,2048]{1,0:T(8,128)(2,1)S(1)}, bf16[128,768]{1,0:T(8,128)(2,1)S(1)}, bf16[128,768]{1,0:T(8,128)(2,...) custom-call(bf16[8,2048]{1,0:T(8,128)(2,1)S(1)} %copy-done.1, bf16[8,2048]{1,0:T(8,128)(2,1)S(1)} %copy-done.2, ...), custom_call_target="tpu_custom_call" | custom-call | tf_op jit(solution)/shard_map/exchange/pallas_call | solution.py:353
  54.2 6.6 %weight_grads.1 = (bf16[8,2048]{1,0:T(8,128)(2,1)}, bf16[8,2048]{1,0:T(8,128)(2,1)}, bf16[1,2048,768]{2,1,0:T(8,128)(2,1)}, bf16[1,2048,768]{2,1,0:T(8,128)(2,1)}, bf16[1,768,2048]{2,1,0:T(8,128)(2,1)}) custom-call(bf16[128,2048]{1,0:T(8,128)(2,1)S(1)} %get-tuple-element.11.x_ref, bf16[128,2048]{1,0:T(8,128)(2,1)S(1)} %get-tuple-element.12.eg_ref, ...), custom_call_target="tpu_custom_call" | custom-call | tf_op jit(solution)/shard_map/weight_grads/pallas_call | solution.py:420
Async XLA Ops:
  0.6 1.9 %copy-start = (bf16[1,2048,768]{2,1,0:T(8,128)(2,1)S(1)}, bf16[1,2048,768]{2,1,0:T(8,128)(2,1)}, u32[]{:S(2)}) copy-start(bf16[1,2048,768]{2,1,0:T(8,128)(2,1)} %gate_hbm.1) | copy-start | bytes 9437188
  2.5 0.8 %copy-start.1 = (bf16[8,2048]{1,0:T(8,128)(2,1)S(1)}, bf16[8,2048]{1,0:T(8,128)(2,1)}, u32[]{:S(2)}) copy-start(bf16[8,2048]{1,0:T(8,128)(2,1)} %tok_ref.1) | copy-start | bytes 98308
  3.3 0.8 %copy-start.2 = (bf16[8,2048]{1,0:T(8,128)(2,1)S(1)}, bf16[8,2048]{1,0:T(8,128)(2,1)}, u32[]{:S(2)}) copy-start(bf16[8,2048]{1,0:T(8,128)(2,1)} %grad_ref.1) | copy-start | bytes 98308
  4.0 0.7 %copy-start.3 = (s32[8,8]{1,0:T(8,128)S(1)}, s32[8,8]{1,0:T(8,128)}, u32[]{:S(2)}) copy-start(s32[8,8]{1,0:T(8,128)} %id_ref.1) | copy-start | bytes 772
  4.7 0.7 %copy-start.4 = (f32[8,8]{1,0:T(8,128)S(1)}, f32[8,8]{1,0:T(8,128)}, u32[]{:S(2)}) copy-start(f32[8,8]{1,0:T(8,128)} %weight_ref.1) | copy-start | bytes 772

commit v2 on v1

--- a/solution.py
+++ b/solution.py
@@ -118,9 +118,10 @@
 
 
 def exchange_kernel(
-    planes,
-    tok_ref, grad_ref, id_ref, weight_ref, gate_hbm, up_hbm, down_hbm,
+    planes, per,
+    tok_hbm, grad_hbm, id_hbm, weight_hbm, gate_hbm, up_hbm, down_hbm,
     x_ref, eg_ref, hidden_ref, gg_ref, ug_ref, sum_ref,
+    tok_ref, grad_ref, id_ref, weight_ref,
     w_gate, w_up, w_down, load_sem,
     msg, scale, part, other, back, back_sib, mid, mid_x, last, last_z,
     z_send, z_recv, x_send, x_recv, s_send, s_recv, y_send, y_recv,
@@ -130,6 +131,8 @@
     ff = w_gate.shape[1]
     top = id_ref.shape[1]
     chunk = 4 * rows
+    groups = planes // per
+    held = per * chunk
     me = lax.axis_index("expert")
     core = me % 2
     side = (me // 2) % 2
@@ -142,10 +145,11 @@
         return {"expert": partner(plane, step) * 4 + side * 2 + core}
 
     loads = []
-    for i, (source, target) in enumerate(
-        ((gate_hbm, w_gate), (up_hbm, w_up), (down_hbm, w_down))
-    ):
-        load = pltpu.make_async_copy(source.at[0], target, load_sem.at[i])
+    for i, (source, target) in enumerate((
+        (tok_hbm, tok_ref), (grad_hbm, grad_ref), (id_hbm, id_ref), (weight_hbm, weight_ref),
+        (gate_hbm.at[0], w_gate), (up_hbm.at[0], w_up), (down_hbm.at[0], w_down),
+    )):
+        load = pltpu.make_async_copy(source, target, load_sem.at[i])
         load.start()
         loads.append(load)
 
@@ -154,6 +158,8 @@
     for peer in peers:
         pl.semaphore_signal(barrier, inc=1, device_id=peer, device_id_type=MESH)
 
+    for load in loads[:4]:
+        load.wait()
     lane = lax.broadcasted_iota(jnp.int32, (rows, LANES), 1)
     dense = jnp.zeros((rows, LANES), jnp.float32)
     chosen = jnp.zeros((rows, LANES), jnp.float32)
@@ -207,7 +213,7 @@
         arrived(msg.at[k, side, 1 - core], s_send.at[k, 0], s_recv.at[k, 0], sibling)
         arrived(msg.at[k, 1 - side, 1 - core], s_send.at[k, 1], s_recv.at[k, 1], sibling)
 
-    def first_half(k):
+    def gather_rows(k):
         mine = lax.broadcasted_iota(jnp.int32, (rows, LANES), 1) == me
         at = k * chunk
         for s in range(2):
@@ -220,48 +226,53 @@
                 body = msg[k, s, c, :, :wide].astype(jnp.float32)
                 ins.append(body[:rows] * mask)
                 grads.append(body[rows:] * weight)
-                j = 2 * s + c
-                scale[k, j * rows:(j + 1) * rows, :] = jnp.broadcast_to(weight, (rows, LANES))
+                first = at + (2 * s + c) * rows
+                scale[first:first + rows, :] = jnp.broadcast_to(weight, (rows, LANES))
             here = slice(at + 2 * s * rows, at + 2 * (s + 1) * rows)
             x_ref[here, :] = jnp.concatenate(ins, axis=0).astype(jnp.bfloat16)
             eg_ref[here, :] = jnp.concatenate(grads, axis=0).astype(jnp.bfloat16)
 
+    def first_half(g, hooks):
         tile = min(256, ff)
-        span = slice(at, at + chunk)
+        span = slice(g * held, (g + 1) * held)
 
         def give(i):
-            send(part.at[k, i], other.at[k, i], y_send.at[k, i], y_recv.at[k, i], pair)
+            send(part.at[g, i], other.at[g, i], y_send.at[g, i], y_recv.at[g, i], pair)
 
         for i, matrix in enumerate((w_gate, w_up)):
-            if k == 0:
-                loads[i].wait()
+            if g == 0:
+                loads[4 + i].wait()
 
             @pl.loop(0, ff // tile)
             def _(n):
                 cols = pl.ds(pl.multiple_of(n * tile, tile), tile)
-                part[k, i, :, cols] = jnp.dot(
+                part[g, i, :, cols] = jnp.dot(
                     x_ref[span, :], matrix[:, cols], preferred_element_type=jnp.float32
                 ).astype(jnp.bfloat16)
 
             give(i)
-        if k == 0:
-            loads[2].wait()
+            for hook in hooks[i]:
+                hook()
+        if g == 0:
+            loads[6].wait()
 
         @pl.loop(0, ff // tile)
         def _(n):
             cols = pl.ds(pl.multiple_of(n * tile, tile), tile)
-            part[k, 2, :, cols] = contract_cols(eg_ref[span, :], w_down[cols, :]).astype(
+            part[g, 2, :, cols] = contract_cols(eg_ref[span, :], w_down[cols, :]).astype(
                 jnp.bfloat16
             )
 
         give(2)
-
-    def second_half(k):
-        span = slice(k * chunk, (k + 1) * chunk)
+        for hook in hooks[2]:
+            hook()
+
+    def second_half(g):
+        span = slice(g * held, (g + 1) * held)
         for i in range(3):
-            arrived(other.at[k, i], y_send.at[k, i], y_recv.at[k, i], pair)
+            arrived(other.at[g, i], y_send.at[g, i], y_recv.at[g, i], pair)
         gate, up_value, hidden_grad = [
-            part[k, i].astype(jnp.float32) + other[k, i].astype(jnp.float32) for i in range(3)
+            part[g, i].astype(jnp.float32) + other[g, i].astype(jnp.float32) for i in range(3)
         ]
         sig = jax.nn.sigmoid(gate)
         silu = gate * sig
@@ -277,18 +288,21 @@
             cols = pl.ds(pl.multiple_of(n * tile, tile), tile)
             out = jnp.dot(
                 hidden_ref[span, :], w_down[:, cols], preferred_element_type=jnp.float32
-            ) * scale[k, :, 0:1]
+            ) * scale[span, 0:1]
             back_in = contract_cols(gg_ref[span, :], w_gate[cols, :]) + contract_cols(
                 ug_ref[span, :], w_up[cols, :]
             )
-            for s in range(2):
-                for c in range(2):
-                    block = slice((2 * s + c) * rows, (2 * s + c + 1) * rows)
-                    back[k, c, s, :, cols] = jnp.concatenate(
-                        [out[block], back_in[block]], axis=0
-                    ).astype(jnp.bfloat16)
-
-        send(back.at[k, 1 - core], back_sib.at[k], r1_send.at[k], r1_recv.at[k], sibling)
+            for p in range(per):
+                for s in range(2):
+                    for c in range(2):
+                        first = p * chunk + (2 * s + c) * rows
+                        block = slice(first, first + rows)
+                        back[g * per + p, c, s, :, cols] = jnp.concatenate(
+                            [out[block], back_in[block]], axis=0
+                        ).astype(jnp.bfloat16)
+
+        for k in range(g * per, (g + 1) * per):
+            send(back.at[k, 1 - core], back_sib.at[k], r1_send.at[k], r1_recv.at[k], sibling)
 
     def sum_core(k):
         arrived(back_sib.at[k], r1_send.at[k], r1_recv.at[k], sibling)
@@ -310,25 +324,31 @@
     for k in range(1, planes):
         send(own, msg.at[k, side, core], z_send.at[k], z_recv.at[k], in_plane(k))
 
-    ahead = min(2, planes - 1)
-    for k in range(planes + ahead):
-        if k < planes:
-            relay(k)
-            if k + 1 < planes:
-                spread(k + 1)
+    for k in range(per):
+        relay(k)
+        if k + 1 < per:
+            spread(k + 1)
+    for g in range(groups):
+        for k in range(g * per, (g + 1) * per):
             gather_end(k)
-            first_half(k)
-        done = k - ahead
-        if done >= 0:
-            second_half(done)
-            if done >= 1:
-                sum_core(done - 1)
-            if done >= 2:
-                sum_side(done - 2)
-    if planes >= 2:
-        sum_side(planes - 2)
-    sum_core(planes - 1)
-    sum_side(planes - 1)
+            gather_rows(k)
+        hooks = [[], [], []]
+        if g + 1 < groups:
+            coming = range((g + 1) * per, (g + 2) * per)
+            hooks[0] = [functools.partial(spread, coming[0])]
+            hooks[1] = [functools.partial(spread, k) for k in coming[1:]]
+            hooks[1].append(functools.partial(relay, coming[0]))
+            hooks[2] = [functools.partial(relay, k) for k in coming[1:]]
+        first_half(g, hooks)
+    for g in range(groups):
+        second_half(g)
+        if g > 0:
+            for k in range((g - 1) * per, g * per):
+                sum_side(k)
+        for k in range(g * per, (g + 1) * per):
+            sum_core(k)
+    for k in range((groups - 1) * per, planes):
+        sum_side(k)
 
     total = last[0].astype(jnp.float32)
     for k in range(1, planes):
@@ -347,11 +367,13 @@
     total = experts * rows
     chunk = 4 * rows
     bf16 = jnp.bfloat16
+    per = max(1, planes // 2)
+    groups = planes // per
     vmem = pl.BlockSpec(memory_space=pltpu.VMEM)
-    hbm = pl.BlockSpec(memory_space=pl.ANY)
+    hbm = pl.BlockSpec(memory_space=pltpu.HBM)
     dma = pltpu.SemaphoreType.DMA
     return pl.pallas_call(
-        functools.partial(exchange_kernel, planes),
+        functools.partial(exchange_kernel, planes, per),
         out_shape=(
             jax.ShapeDtypeStruct((total, wide), bf16),
             jax.ShapeDtypeStruct((total, wide), bf16),
@@ -360,17 +382,21 @@
             jax.ShapeDtypeStruct((total, ff), bf16),
             jax.ShapeDtypeStruct((2 * rows, wide), bf16),
         ),
-        in_specs=[vmem] * 4 + [hbm] * 3,
+        in_specs=[hbm] * 7,
         out_specs=(vmem,) * 6,
         scratch_shapes=[
+            pltpu.VMEM((rows, wide), bf16),
+            pltpu.VMEM((rows, wide), bf16),
+            pltpu.VMEM(expert_ids.shape, expert_ids.dtype),
+            pltpu.VMEM(route_weights.shape, route_weights.dtype),
             pltpu.VMEM((wide, ff), bf16),
             pltpu.VMEM((wide, ff), bf16),
             pltpu.VMEM((ff, wide), bf16),
-            dma((3,)),
+            dma((7,)),
             pltpu.VMEM((planes, 2, 2, 2 * rows, wide + 2 * LANES), bf16),
-            pltpu.VMEM((planes, chunk, LANES), jnp.float32),
-            pltpu.VMEM((planes, 3, chunk, ff), bf16),
-            pltpu.VMEM((planes, 3, chunk, ff), bf16),
+            pltpu.VMEM((total, LANES), jnp.float32),
+            pltpu.VMEM((groups, 3, per * chunk, ff), bf16),
+            pltpu.VMEM((groups, 3, per * chunk, ff), bf16),
             pltpu.VMEM((planes, 2, 2, 2 * rows, wide), bf16),
             pltpu.VMEM((planes, 2, 2 * rows, wide), bf16),
             pltpu.VMEM((planes, 2, 2 * rows, wide), bf16),
@@ -380,16 +406,19 @@
             dma((planes,)), dma((planes,)),
             dma((planes,)), dma((planes,)),
             dma((planes, 2)), dma((planes, 2)),
-            dma((planes, 3)), dma((planes, 3)),
+            dma((groups, 3)), dma((groups, 3)),
             dma((planes,)), dma((planes,)),
             dma((planes,)), dma((planes,)),
             dma((planes,)), dma((planes,)),
         ],
         compiler_params=pltpu.CompilerParams(
-            collective_id=0, has_side_effects=True, vmem_limit_bytes=48 * 1024 * 1024
+            collective_id=0, has_side_effects=True, vmem_limit_bytes=40 * 1024 * 1024
         ),
         name="exchange",
-    )(tokens, grad_out, expert_ids, route_weights, w_gate, w_up, w_down)
+    )(*[
+        pltpu.with_memory_space_constraint(operand, pltpu.HBM)
+        for operand in (tokens, grad_out, expert_ids, route_weights, w_gate, w_up, w_down)
+    ])
 
 
 def weights_kernel(x_ref, eg_ref, hidden_ref, gg_ref, ug_ref, sum_ref,

time: 61.2 us -> 52 us (0.85)
  local copies, waits for them, and re-layouts: 4.77 us -> 0 us
  Pallas kernels: 55.4 us -> 51.2 us
    unnamed x10 -> x0, local copies, waits for them, and re-layouts: 4.77 us -> none
    pallas_call x1, Pallas kernels: 48.8 us -> 44.6 us  [exchange(): pl.pallas_call(functools.partial(exchange_kernel, planes, per), out_shape...]
where the time goes in v2:
time: 52 us; the launch traced here: 51.9 us
  Pallas kernels  51.2 us (98%)
  between operations  0.64 us (1%)
    pallas_call x1, Pallas kernels, exchange(): pl.pallas_call(functools.partial(exchange_kernel, planes, per), out_shape...  44.6 us
    pallas_call x1, Pallas kernels, weight_grads(): pl.pallas_call(weights_kernel, grid=(wide // tile,), out_shape=(jax.Shape...  6.63 us

profile of v2, /device:TPU:0, one launch (start us, length us, event | category | flops | bytes accessed | tf_op | source)
XLA Modules:
  0.0 51.9 jit_solution(9390728820553366675)
XLA Ops:
  0.6 44.6 %exchange.1 = (bf16[128,2048]{1,0:T(8,128)(2,1)S(1)}, bf16[128,2048]{1,0:T(8,128)(2,1)S(1)}, bf16[128,768]{1,0:T(8,128)(2,1)S(1)}, bf16[128,768]{1,0:T(8,128)(2,...) custom-call(bf16[8,2048]{1,0:T(8,128)(2,1)} %tok_hbm.1, bf16[8,2048]{1,0:T(8,128)(2,1)} %grad_hbm.1, ...), custom_call_target="tpu_custom_call" | custom-call | tf_op jit(solution)/shard_map/exchange/pallas_call | solution.py:375
  45.3 6.6 %weight_grads.1 = (bf16[8,2048]{1,0:T(8,128)(2,1)}, bf16[8,2048]{1,0:T(8,128)(2,1)}, bf16[1,2048,768]{2,1,0:T(8,128)(2,1)}, bf16[1,2048,768]{2,1,0:T(8,128)(2,1)}, bf16[1,768,2048]{2,1,0:T(8,128)(2,1)}) custom-call(bf16[128,2048]{1,0:T(8,128)(2,1)S(1)} %get-tuple-element.11.x_ref, bf16[128,2048]{1,0:T(8,128)(2,1)S(1)} %get-tuple-element.12.eg_ref, ...), custom_call_target="tpu_custom_call" | custom-call | tf_op jit(solution)/shard_map/weight_grads/pallas_call | solution.py:449

commit v3 on v2

--- a/solution.py
+++ b/solution.py
@@ -319,36 +319,36 @@
         if k > 0:
             send(last.at[k], last_z.at[k], r3_send.at[k], r3_recv.at[k], in_plane(k))
 
+    order = [0] + list(range(2, planes)) + list(range(1, min(2, planes)))
     own = msg.at[0, side, core]
     spread(0)
-    for k in range(1, planes):
+    for k in order[1:]:
         send(own, msg.at[k, side, core], z_send.at[k], z_recv.at[k], in_plane(k))
-
-    for k in range(per):
-        relay(k)
-        if k + 1 < per:
-            spread(k + 1)
-    for g in range(groups):
-        for k in range(g * per, (g + 1) * per):
-            gather_end(k)
-            gather_rows(k)
+    relay(0)
+    if planes > 1:
+        spread(order[1])
+
+    def begin(i):
+        gather_end(order[i])
+        gather_rows(order[i])
         hooks = [[], [], []]
-        if g + 1 < groups:
-            coming = range((g + 1) * per, (g + 2) * per)
-            hooks[0] = [functools.partial(spread, coming[0])]
-            hooks[1] = [functools.partial(spread, k) for k in coming[1:]]
-            hooks[1].append(functools.partial(relay, coming[0]))
-            hooks[2] = [functools.partial(relay, k) for k in coming[1:]]
-        first_half(g, hooks)
-    for g in range(groups):
-        second_half(g)
-        if g > 0:
-            for k in range((g - 1) * per, g * per):
-                sum_side(k)
-        for k in range(g * per, (g + 1) * per):
-            sum_core(k)
-    for k in range((groups - 1) * per, planes):
-        sum_side(k)
+        if i + 1 < planes:
+            hooks[0] = [functools.partial(relay, order[i + 1])]
+        if i + 2 < planes:
+            hooks[2] = [functools.partial(spread, order[i + 2])]
+        first_half(order[i], hooks)
+
+    ahead = min(3, planes)
+    for i in range(ahead):
+        begin(i)
+    for i in range(planes):
+        second_half(order[i])
+        if i + ahead < planes:
+            begin(i + ahead)
+        if i > 0:
+            sum_side(order[i - 1])
+        sum_core(order[i])
+    sum_side(order[-1])
 
     total = last[0].astype(jnp.float32)
     for k in range(1, planes):
@@ -367,7 +367,7 @@
     total = experts * rows
     chunk = 4 * rows
     bf16 = jnp.bfloat16
-    per = max(1, planes // 2)
+    per = 1
     groups = planes // per
     vmem = pl.BlockSpec(memory_space=pltpu.VMEM)
     hbm = pl.BlockSpec(memory_space=pltpu.HBM)

time: 52 us -> 60.1 us (1.16)
  Pallas kernels: 51.2 us -> 59.3 us
    pallas_call x1, Pallas kernels: 44.6 us -> 52.7 us  [exchange(): pl.pallas_call(functools.partial(exchange_kernel, planes, per), out_shape...]
where the time goes in v3:
time: 60.1 us; the launch traced here: 60 us
  Pallas kernels  59.3 us (99%)
  between operations  0.64 us (1%)
    pallas_call x1, Pallas kernels, exchange(): pl.pallas_call(functools.partial(exchange_kernel, planes, per), out_shape...  52.7 us
    pallas_call x1, Pallas kernels, weight_grads(): pl.pallas_call(weights_kernel, grid=(wide // tile,), out_shape=(jax.Shape...  6.63 us

profile of v3, /device:TPU:0, one launch (start us, length us, event | category | flops | bytes accessed | tf_op | source)
XLA Modules:
  0.0 60.0 jit_solution(13130701519617406685)
XLA Ops:
  0.6 52.7 %exchange.1 = (bf16[128,2048]{1,0:T(8,128)(2,1)S(1)}, bf16[128,2048]{1,0:T(8,128)(2,1)S(1)}, bf16[128,768]{1,0:T(8,128)(2,1)S(1)}, bf16[128,768]{1,0:T(8,128)(2,...) custom-call(bf16[8,2048]{1,0:T(8,128)(2,1)} %tok_hbm.1, bf16[8,2048]{1,0:T(8,128)(2,1)} %grad_hbm.1, ...), custom_call_target="tpu_custom_call" | custom-call | tf_op jit(solution)/shard_map/exchange/pallas_call | solution.py:375
  53.3 6.6 %weight_grads.1 = (bf16[8,2048]{1,0:T(8,128)(2,1)}, bf16[8,2048]{1,0:T(8,128)(2,1)}, bf16[1,2048,768]{2,1,0:T(8,128)(2,1)}, bf16[1,2048,768]{2,1,0:T(8,128)(2,1)}, bf16[1,768,2048]{2,1,0:T(8,128)(2,1)}) custom-call(bf16[128,2048]{1,0:T(8,128)(2,1)S(1)} %get-tuple-element.11.x_ref, bf16[128,2048]{1,0:T(8,128)(2,1)S(1)} %get-tuple-element.12.eg_ref, ...), custom_call_target="tpu_custom_call" | custom-call | tf_op jit(solution)/shard_map/weight_grads/pallas_call | solution.py:449

commit v4 on v2

--- a/solution.py
+++ b/solution.py
@@ -233,7 +233,7 @@
             eg_ref[here, :] = jnp.concatenate(grads, axis=0).astype(jnp.bfloat16)
 
     def first_half(g, hooks):
-        tile = min(256, ff)
+        tile = ff
         span = slice(g * held, (g + 1) * held)
 
         def give(i):
@@ -267,57 +267,80 @@
         for hook in hooks[2]:
             hook()
 
-    def second_half(g):
-        span = slice(g * held, (g + 1) * held)
-        for i in range(3):
-            arrived(other.at[g, i], y_send.at[g, i], y_recv.at[g, i], pair)
-        gate, up_value, hidden_grad = [
-            part[g, i].astype(jnp.float32) + other[g, i].astype(jnp.float32) for i in range(3)
-        ]
-        sig = jax.nn.sigmoid(gate)
-        silu = gate * sig
-        hidden_ref[span, :] = (silu * up_value).astype(jnp.bfloat16)
-        gg_ref[span, :] = (
-            hidden_grad * up_value * sig * (1.0 + gate * (1.0 - sig))
-        ).astype(jnp.bfloat16)
-        ug_ref[span, :] = (hidden_grad * silu).astype(jnp.bfloat16)
-        tile = min(512, wide)
-
-        @pl.loop(0, wide // tile)
+    half = wide // 2
+    tile_out = min(512, half)
+
+    def give_back(kind, g, product):
+        @pl.loop(0, half // tile_out)
         def _(n):
-            cols = pl.ds(pl.multiple_of(n * tile, tile), tile)
-            out = jnp.dot(
-                hidden_ref[span, :], w_down[:, cols], preferred_element_type=jnp.float32
-            ) * scale[span, 0:1]
-            back_in = contract_cols(gg_ref[span, :], w_gate[cols, :]) + contract_cols(
-                ug_ref[span, :], w_up[cols, :]
-            )
+            cols = pl.ds(pl.multiple_of(n * tile_out, tile_out), tile_out)
+            high = pl.ds(pl.multiple_of(half + n * tile_out, tile_out), tile_out)
+            left, right = product(cols), product(high)
             for p in range(per):
                 for s in range(2):
                     for c in range(2):
                         first = p * chunk + (2 * s + c) * rows
                         block = slice(first, first + rows)
-                        back[g * per + p, c, s, :, cols] = jnp.concatenate(
-                            [out[block], back_in[block]], axis=0
+                        back[kind, g, c, s, p, :, cols] = jnp.concatenate(
+                            [left[block], right[block]], axis=0
                         ).astype(jnp.bfloat16)
 
-        for k in range(g * per, (g + 1) * per):
-            send(back.at[k, 1 - core], back_sib.at[k], r1_send.at[k], r1_recv.at[k], sibling)
-
-    def sum_core(k):
-        arrived(back_sib.at[k], r1_send.at[k], r1_recv.at[k], sibling)
-        mid[k] = (
-            back[k, core].astype(jnp.float32) + back_sib[k].astype(jnp.float32)
+        send(
+            back.at[kind, g, 1 - core], back_sib.at[kind, g],
+            r1_send.at[kind, g], r1_recv.at[kind, g], sibling,
+        )
+
+    def summed(g, i):
+        arrived(other.at[g, i], y_send.at[g, i], y_recv.at[g, i], pair)
+        return part[g, i].astype(jnp.float32) + other[g, i].astype(jnp.float32)
+
+    def outputs(g):
+        span = slice(g * held, (g + 1) * held)
+        gate, up_value = summed(g, 0), summed(g, 1)
+        hidden_ref[span, :] = (gate * jax.nn.sigmoid(gate) * up_value).astype(jnp.bfloat16)
+        give_back(0, g, lambda cols: jnp.dot(
+            hidden_ref[span, :], w_down[:, cols], preferred_element_type=jnp.float32
+        ) * scale[span, 0:1])
+
+    def inputs(g):
+        span = slice(g * held, (g + 1) * held)
+        hidden_grad = summed(g, 2)
+        gate, up_value = [
+            part[g, i].astype(jnp.float32) + other[g, i].astype(jnp.float32) for i in range(2)
+        ]
+        gg_ref[span, :], ug_ref[span, :] = gate_grads(hidden_grad, gate, up_value)
+        give_back(1, g, lambda cols: contract_cols(gg_ref[span, :], w_gate[cols, :])
+                  + contract_cols(ug_ref[span, :], w_up[cols, :]))
+
+    def sum_core(kind, g):
+        arrived(back_sib.at[kind, g], r1_send.at[kind, g], r1_recv.at[kind, g], sibling)
+        mid[kind, g] = (
+            back[kind, g, core].astype(jnp.float32) + back_sib[kind, g].astype(jnp.float32)
         ).astype(jnp.bfloat16)
-        send(mid.at[k, 1 - side], mid_x.at[k], r2_send.at[k], r2_recv.at[k], across)
-
-    def sum_side(k):
-        arrived(mid_x.at[k], r2_send.at[k], r2_recv.at[k], across)
-        last[k] = (
-            mid[k, side].astype(jnp.float32) + mid_x[k].astype(jnp.float32)
+        send(
+            mid.at[kind, g, 1 - side], mid_x.at[kind, g],
+            r2_send.at[kind, g], r2_recv.at[kind, g], across,
+        )
+
+    def sum_side(kind, g):
+        arrived(mid_x.at[kind, g], r2_send.at[kind, g], r2_recv.at[kind, g], across)
+        last[kind, g] = (
+            mid[kind, g, side].astype(jnp.float32) + mid_x[kind, g].astype(jnp.float32)
         ).astype(jnp.bfloat16)
-        if k > 0:
-            send(last.at[k], last_z.at[k], r3_send.at[k], r3_recv.at[k], in_plane(k))
+        for p in range(per):
+            k = g * per + p
+            if k > 0:
+                send(
+                    last.at[kind, g, p], last_z.at[kind, k],
+                    r3_send.at[kind, k], r3_recv.at[kind, k], in_plane(k),
+                )
+
+    def finish(kind):
+        total = last[kind, 0, 0].astype(jnp.float32)
+        for k in range(1, planes):
+            arrived(last_z.at[kind, k], r3_send.at[kind, k], r3_recv.at[kind, k], in_plane(k))
+            total = total + last_z[kind, k].astype(jnp.float32)
+        sum_ref[kind] = total.astype(jnp.bfloat16)
 
     own = msg.at[0, side, core]
     spread(0)
@@ -341,20 +364,19 @@
             hooks[2] = [functools.partial(relay, k) for k in coming[1:]]
         first_half(g, hooks)
     for g in range(groups):
-        second_half(g)
+        outputs(g)
         if g > 0:
-            for k in range((g - 1) * per, g * per):
-                sum_side(k)
-        for k in range(g * per, (g + 1) * per):
-            sum_core(k)
-    for k in range((groups - 1) * per, planes):
-        sum_side(k)
-
-    total = last[0].astype(jnp.float32)
-    for k in range(1, planes):
-        arrived(last_z.at[k], r3_send.at[k], r3_recv.at[k], in_plane(k))
-        total = total + last_z[k].astype(jnp.float32)
-    sum_ref[...] = total.astype(jnp.bfloat16)
+            sum_core(1, g - 1)
+            sum_side(0, g - 1)
+        inputs(g)
+        if g > 0:
+            sum_side(1, g - 1)
+        sum_core(0, g)
+    sum_side(0, groups - 1)
+    sum_core(1, groups - 1)
+    sum_side(1, groups - 1)
+    finish(0)
+    finish(1)
     for copy in sends:
         copy.wait_send()
 
@@ -380,7 +402,7 @@
             jax.ShapeDtypeStruct((total, ff), bf16),
             jax.ShapeDtypeStruct((total, ff), bf16),
             jax.ShapeDtypeStruct((total, ff), bf16),
-            jax.ShapeDtypeStruct((2 * rows, wide), bf16),
+            jax.ShapeDtypeStruct((2, 2 * rows, wide // 2), bf16),
         ),
         in_specs=[hbm] * 7,
         out_specs=(vmem,) * 6,
@@ -397,19 +419,19 @@
             pltpu.VMEM((total, LANES), jnp.float32),
             pltpu.VMEM((groups, 3, per * chunk, ff), bf16),
             pltpu.VMEM((groups, 3, per * chunk, ff), bf16),
-            pltpu.VMEM((planes, 2, 2, 2 * rows, wide), bf16),
-            pltpu.VMEM((planes, 2, 2 * rows, wide), bf16),
-            pltpu.VMEM((planes, 2, 2 * rows, wide), bf16),
-            pltpu.VMEM((planes, 2 * rows, wide), bf16),
-            pltpu.VMEM((planes, 2 * rows, wide), bf16),
-            pltpu.VMEM((planes, 2 * rows, wide), bf16),
+            pltpu.VMEM((2, groups, 2, 2, per, 2 * rows, wide // 2), bf16),
+            pltpu.VMEM((2, groups, 2, per, 2 * rows, wide // 2), bf16),
+            pltpu.VMEM((2, groups, 2, per, 2 * rows, wide // 2), bf16),
+            pltpu.VMEM((2, groups, per, 2 * rows, wide // 2), bf16),
+            pltpu.VMEM((2, groups, per, 2 * rows, wide // 2), bf16),
+            pltpu.VMEM((2, planes, 2 * rows, wide // 2), bf16),
             dma((planes,)), dma((planes,)),
             dma((planes,)), dma((planes,)),
             dma((planes, 2)), dma((planes, 2)),
             dma((groups, 3)), dma((groups, 3)),
-            dma((planes,)), dma((planes,)),
-            dma((planes,)), dma((planes,)),
-            dma((planes,)), dma((planes,)),
+            dma((2, groups)), dma((2, groups)),
+            dma((2, groups)), dma((2, groups)),
+            dma((2, planes)), dma((2, planes)),
         ],
         compiler_params=pltpu.CompilerParams(
             collective_id=0, has_side_effects=True, vmem_limit_bytes=40 * 1024 * 1024
@@ -430,15 +452,17 @@
 
     @pl.when(pl.program_id(0) == 0)
     def _():
-        both = sum_ref[...].astype(jnp.float32)
-        out_ref[...] = both[:rows].astype(jnp.bfloat16)
-        in_ref[...] = both[rows:].astype(jnp.bfloat16)
+        for kind, ref in enumerate((out_ref, in_ref)):
+            both = sum_ref[kind].astype(jnp.float32)
+            half = both.shape[1]
+            ref[:, :half] = both[:rows].astype(jnp.bfloat16)
+            ref[:, half:] = both[rows:].astype(jnp.bfloat16)
 
 
 def weight_grads(x, eg, hidden, gg, ug, sums):
     total, wide = x.shape
     ff = hidden.shape[1]
-    rows = sums.shape[0] // 2
+    rows = sums.shape[1] // 2
     tile = min(256, wide)
     bf16 = jnp.bfloat16
 
@@ -456,7 +480,7 @@
             jax.ShapeDtypeStruct((1, wide, ff), bf16),
             jax.ShapeDtypeStruct((1, ff, wide), bf16),
         ),
-        in_specs=[cols, cols] + [whole((total, ff))] * 3 + [whole((2 * rows, wide))],
+        in_specs=[cols, cols] + [whole((total, ff))] * 3 + [whole((2, 2 * rows, wide // 2))],
         out_specs=(
             whole((rows, wide)),
             whole((rows, wide)),

time: 52 us -> 51.2 us (0.985)
  Pallas kernels: 51.2 us -> 50.4 us
    pallas_call x1, Pallas kernels: 44.6 us -> 43.7 us  [exchange(): pl.pallas_call(functools.partial(exchange_kernel, planes, per), out_shape...]
where the time goes in v4:
time: 51.2 us; the launch traced here: 51 us
  Pallas kernels  50.4 us (98%)
  between operations  0.64 us (1%)
    pallas_call x1, Pallas kernels, exchange(): pl.pallas_call(functools.partial(exchange_kernel, planes, per), out_shape...  43.7 us
    pallas_call x1, Pallas kernels, weight_grads(): pl.pallas_call(weights_kernel, grid=(wide // tile,), out_shape=(jax.Shape...  6.64 us

profile of v4, /device:TPU:0, one launch (start us, length us, event | category | flops | bytes accessed | tf_op | source)
XLA Modules:
  0.0 51.0 jit_solution(14180071241851286387)
XLA Ops:
  0.6 43.7 %exchange.1 = (bf16[128,2048]{1,0:T(8,128)(2,1)S(1)}, bf16[128,2048]{1,0:T(8,128)(2,1)S(1)}, bf16[128,768]{1,0:T(8,128)(2,1)S(1)}, bf16[128,768]{1,0:T(8,128)(2,...) custom-call(bf16[8,2048]{1,0:T(8,128)(2,1)} %tok_hbm.1, bf16[8,2048]{1,0:T(8,128)(2,1)} %grad_hbm.1, ...), custom_call_target="tpu_custom_call" | custom-call | tf_op jit(solution)/shard_map/exchange/pallas_call | solution.py:397
  44.4 6.6 %weight_grads.1 = (bf16[8,2048]{1,0:T(8,128)(2,1)}, bf16[8,2048]{1,0:T(8,128)(2,1)}, bf16[1,2048,768]{2,1,0:T(8,128)(2,1)}, bf16[1,2048,768]{2,1,0:T(8,128)(2,1)}, bf16[1,768,2048]{2,1,0:T(8,128)(2,1)}) custom-call(bf16[128,2048]{1,0:T(8,128)(2,1)S(1)} %get-tuple-element.11.x_ref, bf16[128,2048]{1,0:T(8,128)(2,1)S(1)} %get-tuple-element.12.eg_ref, ...), custom_call_target="tpu_custom_call" | custom-call | tf_op jit(solution)/shard_map/weight_grads/pallas_call | solution.py:473

commit v5 on v4

--- a/solution.py
+++ b/solution.py
@@ -120,7 +120,8 @@
 def exchange_kernel(
     planes, per,
     tok_hbm, grad_hbm, id_hbm, weight_hbm, gate_hbm, up_hbm, down_hbm,
-    x_ref, eg_ref, hidden_ref, gg_ref, ug_ref, sum_ref,
+    sum_ref, gate_ref, up_ref, down_ref,
+    x_ref, eg_ref, hidden_ref, gg_ref, ug_ref,
     tok_ref, grad_ref, id_ref, weight_ref,
     w_gate, w_up, w_down, load_sem,
     msg, scale, part, other, back, back_sib, mid, mid_x, last, last_z,
@@ -363,6 +364,32 @@
             hooks[1].append(functools.partial(relay, coming[0]))
             hooks[2] = [functools.partial(relay, k) for k in coming[1:]]
         first_half(g, hooks)
+    step = min(256, wide)
+
+    def down_grad():
+        hidden_t = hidden_ref[...].T
+
+        @pl.loop(0, wide // step)
+        def _(n):
+            cols = pl.ds(pl.multiple_of(n * step, step), step)
+            down_ref[:, cols] = jnp.dot(
+                hidden_t, eg_ref[:, cols], preferred_element_type=jnp.float32
+            ).astype(jnp.bfloat16)
+
+    def in_grads(part_of):
+        pieces = wide // step // 2
+
+        @pl.loop(part_of * pieces, (part_of + 1) * pieces)
+        def _(n):
+            cols = pl.ds(pl.multiple_of(n * step, step), step)
+            x_t = x_ref[:, cols].T
+            gate_ref[cols, :] = jnp.dot(
+                x_t, gg_ref[...], preferred_element_type=jnp.float32
+            ).astype(jnp.bfloat16)
+            up_ref[cols, :] = jnp.dot(
+                x_t, ug_ref[...], preferred_element_type=jnp.float32
+            ).astype(jnp.bfloat16)
+
     for g in range(groups):
         outputs(g)
         if g > 0:
@@ -372,9 +399,12 @@
         if g > 0:
             sum_side(1, g - 1)
         sum_core(0, g)
+    sum_core(1, groups - 1)
     sum_side(0, groups - 1)
-    sum_core(1, groups - 1)
+    down_grad()
     sum_side(1, groups - 1)
+    in_grads(0)
+    in_grads(1)
     finish(0)
     finish(1)
     for copy in sends:
@@ -397,16 +427,19 @@
     return pl.pallas_call(
         functools.partial(exchange_kernel, planes, per),
         out_shape=(
-            jax.ShapeDtypeStruct((total, wide), bf16),
-            jax.ShapeDtypeStruct((total, wide), bf16),
-            jax.ShapeDtypeStruct((total, ff), bf16),
-            jax.ShapeDtypeStruct((total, ff), bf16),
-            jax.ShapeDtypeStruct((total, ff), bf16),
             jax.ShapeDtypeStruct((2, 2 * rows, wide // 2), bf16),
+            jax.ShapeDtypeStruct((wide, ff), bf16),
+            jax.ShapeDtypeStruct((wide, ff), bf16),
+            jax.ShapeDtypeStruct((ff, wide), bf16),
         ),
         in_specs=[hbm] * 7,
-        out_specs=(vmem,) * 6,
+        out_specs=(vmem,) * 4,
         scratch_shapes=[
+            pltpu.VMEM((total, wide), bf16),
+            pltpu.VMEM((total, wide), bf16),
+            pltpu.VMEM((total, ff), bf16),
+            pltpu.VMEM((total, ff), bf16),
+            pltpu.VMEM((total, ff), bf16),
             pltpu.VMEM((rows, wide), bf16),
             pltpu.VMEM((rows, wide), bf16),
             pltpu.VMEM(expert_ids.shape, expert_ids.dtype),
@@ -443,36 +476,40 @@
     ])
 
 
-def weights_kernel(x_ref, eg_ref, hidden_ref, gg_ref, ug_ref, sum_ref,
-                   out_ref, in_ref, gate_ref, up_ref, down_ref):
+PIECES = 4
+
+
+def store_kernel(sum_ref, gate_in, up_in, down_in,
+                 out_ref, in_ref, gate_ref, up_ref, down_ref, sems):
+    copies = []
+    for i, (source, target) in enumerate(
+        ((down_in, down_ref), (gate_in, gate_ref), (up_in, up_ref))
+    ):
+        size = source.shape[0] // PIECES
+        for j in range(PIECES):
+            piece = pl.ds(j * size, size)
+            copy = pltpu.make_async_copy(source.at[piece], target.at[0, piece], sems.at[i, j])
+            copy.start()
+            copies.append(copy)
     rows = out_ref.shape[0]
-    gate_ref[0] = contract_rows(x_ref[...], gg_ref[...]).astype(jnp.bfloat16)
-    up_ref[0] = contract_rows(x_ref[...], ug_ref[...]).astype(jnp.bfloat16)
-    down_ref[0] = contract_rows(hidden_ref[...], eg_ref[...]).astype(jnp.bfloat16)
-
-    @pl.when(pl.program_id(0) == 0)
-    def _():
-        for kind, ref in enumerate((out_ref, in_ref)):
-            both = sum_ref[kind].astype(jnp.float32)
-            half = both.shape[1]
-            ref[:, :half] = both[:rows].astype(jnp.bfloat16)
-            ref[:, half:] = both[rows:].astype(jnp.bfloat16)
-
-
-def weight_grads(x, eg, hidden, gg, ug, sums):
-    total, wide = x.shape
-    ff = hidden.shape[1]
+    for kind, ref in enumerate((out_ref, in_ref)):
+        both = sum_ref[kind].astype(jnp.float32)
+        half = both.shape[1]
+        ref[:, :half] = both[:rows].astype(jnp.bfloat16)
+        ref[:, half:] = both[rows:].astype(jnp.bfloat16)
+    for copy in copies:
+        copy.wait()
+
+
+def store(sums, gate, up, down):
     rows = sums.shape[1] // 2
-    tile = min(256, wide)
+    wide, ff = gate.shape
     bf16 = jnp.bfloat16
-
-    def whole(shape):
-        return pl.BlockSpec(shape, lambda n: (0,) * len(shape))
-
-    cols = pl.BlockSpec((total, tile), lambda n: (0, n))
+    vmem = pl.BlockSpec(memory_space=pltpu.VMEM)
+    anywhere = pl.BlockSpec(memory_space=pl.ANY)
+    hbm = pl.BlockSpec(memory_space=pltpu.HBM)
     return pl.pallas_call(
-        weights_kernel,
-        grid=(wide // tile,),
+        store_kernel,
         out_shape=(
             jax.ShapeDtypeStruct((rows, wide), bf16),
             jax.ShapeDtypeStruct((rows, wide), bf16),
@@ -480,17 +517,12 @@
             jax.ShapeDtypeStruct((1, wide, ff), bf16),
             jax.ShapeDtypeStruct((1, ff, wide), bf16),
         ),
-        in_specs=[cols, cols] + [whole((total, ff))] * 3 + [whole((2, 2 * rows, wide // 2))],
-        out_specs=(
-            whole((rows, wide)),
-            whole((rows, wide)),
-            pl.BlockSpec((1, tile, ff), lambda n: (0, n, 0)),
-            pl.BlockSpec((1, tile, ff), lambda n: (0, n, 0)),
-            pl.BlockSpec((1, ff, tile), lambda n: (0, 0, n)),
-        ),
-        compiler_params=pltpu.CompilerParams(vmem_limit_bytes=32 * 1024 * 1024),
-        name="weight_grads",
-    )(x, eg, hidden, gg, ug, sums)
+        in_specs=[vmem] + [anywhere] * 3,
+        out_specs=(vmem, vmem, hbm, hbm, hbm),
+        scratch_shapes=[pltpu.SemaphoreType.DMA((3, PIECES))],
+        compiler_params=pltpu.CompilerParams(vmem_limit_bytes=16 * 1024 * 1024),
+        name="store",
+    )(sums, gate, up, down)
 
 
 def local(tokens, expert_ids, route_weights, w_gate, w_up, w_down, grad_out):
@@ -506,7 +538,7 @@
     )
     if not fits:
         return general(tokens, expert_ids, route_weights, w_gate, w_up, w_down, grad_out)
-    return weight_grads(
+    return store(
         *exchange(tokens, expert_ids, route_weights, w_gate, w_up, w_down, grad_out)
     )
 

time: 51.2 us -> 48.4 us (0.945)
  Pallas kernels: 50.4 us -> 47.7 us
    pallas_call x1, Pallas kernels: 6.64 us -> 4.35 us  [store(): pl.pallas_call(store_kernel, out_shape=(jax.ShapeDtypeStruct((rows, wide)...]
where the time goes in v5:
time: 48.4 us; the launch traced here: 48.3 us
  Pallas kernels  47.7 us (99%)
  between operations  0.64 us (1%)
    pallas_call x1, Pallas kernels, exchange(): pl.pallas_call(functools.partial(exchange_kernel, planes, per), out_shape...  43.3 us
    pallas_call x1, Pallas kernels, store(): pl.pallas_call(store_kernel, out_shape=(jax.ShapeDtypeStruct((rows, wide)...  4.35 us

profile of v5, /device:TPU:0, one launch (start us, length us, event | category | flops | bytes accessed | tf_op | source)
XLA Modules:
  0.0 48.3 jit_solution(10953960422012415858)
XLA Ops:
  0.6 43.3 %exchange.1 = (bf16[2,16,1024]{2,1,0:T(8,128)(2,1)S(1)}, bf16[2048,768]{1,0:T(8,128)(2,1)S(1)}, bf16[2048,768]{1,0:T(8,128)(2,1)S(1)}, bf16[768,2048]{1,0:T(8,128)(2,1)S(1)}) custom-call(bf16[8,2048]{1,0:T(8,128)(2,1)} %tok_hbm.1, bf16[8,2048]{1,0:T(8,128)(2,1)} %grad_hbm.1, s32[8,8]{1,0:T(8,128)} %id_hbm.1, f32[8,8]{1,0:T(8,128)} %weight_hbm.1, ...), custom_call_target="tpu_custom_call" | custom-call | tf_op jit(solution)/shard_map/exchange/pallas_call | solution.py:427
  43.9 4.3 %store.1 = (bf16[8,2048]{1,0:T(8,128)(2,1)}, bf16[8,2048]{1,0:T(8,128)(2,1)}, bf16[1,2048,768]{2,1,0:T(8,128)(2,1)}, bf16[1,2048,768]{2,1,0:T(8,128)(2,1)}, bf16[1,768,2048]{2,1,0:T(8,128)(2,1)}) custom-call(bf16[2,16,1024]{2,1,0:T(8,128)(2,1)S(1)} %get-tuple-element.9.sum_ref, bf16[2048,768]{1,0:T(8,128)(2,1)S(1)} %get-tuple-element.10.gate_in, ...), custom_call_target="tpu_custom_call" | custom-call | tf_op jit(solution)/shard_map/store/pallas_call | solution.py:511

commit v6 on v5

--- a/solution.py
+++ b/solution.py
@@ -161,24 +161,29 @@
 
     for load in loads[:4]:
         load.wait()
+    half = wide // 2
     lane = lax.broadcasted_iota(jnp.int32, (rows, LANES), 1)
     dense = jnp.zeros((rows, LANES), jnp.float32)
     chosen = jnp.zeros((rows, LANES), jnp.float32)
     for k in range(top):
-        hit = id_ref[:, k:k + 1] == lane
+        hit = id_ref[:, k:k + 1] == lane % (LANES // 2)
         dense = dense + jnp.where(hit, weight_ref[:, k:k + 1], 0.0)
         chosen = chosen + jnp.where(hit, 1.0, 0.0)
     high = dense.astype(jnp.bfloat16).astype(jnp.float32)
     middle = (dense - high).astype(jnp.bfloat16).astype(jnp.float32)
     low = dense - high - middle
-    both = jnp.concatenate(
-        [tok_ref[...].astype(jnp.float32), grad_ref[...].astype(jnp.float32)], axis=0
-    )
-    extra_a = jnp.concatenate([high, low], axis=0)
-    extra_b = jnp.concatenate([middle, chosen], axis=0)
-    msg[0, side, core, :, :wide] = both.astype(jnp.bfloat16)
-    msg[0, side, core, :, wide:wide + LANES] = extra_a.astype(jnp.bfloat16)
-    msg[0, side, core, :, wide + LANES:] = extra_b.astype(jnp.bfloat16)
+    extras = (
+        (chosen, jnp.zeros_like(chosen)),
+        (jnp.where(lane < LANES // 2, high, middle), low),
+    )
+    for kind, ref in enumerate((tok_ref, grad_ref)):
+        body = ref[...].astype(jnp.float32)
+        msg[kind, 0, side, core, :, :half] = jnp.concatenate(
+            [body[:, :half], body[:, half:]], axis=0
+        ).astype(jnp.bfloat16)
+        msg[kind, 0, side, core, :, half:] = jnp.concatenate(
+            extras[kind], axis=0
+        ).astype(jnp.bfloat16)
 
     pl.semaphore_wait(barrier, len(peers))
 
@@ -198,40 +203,46 @@
             device_id=device, device_id_type=MESH,
         ).wait_recv()
 
-    def spread(k):
-        own = msg.at[k, side, core]
+    def spread(kind, k):
+        own = msg.at[kind, k, side, core]
         if k > 0:
-            arrived(own, z_send.at[k], z_recv.at[k], in_plane(k))
-        send(own, own, x_send.at[k], x_recv.at[k], across)
-        send(own, own, s_send.at[k, 0], s_recv.at[k, 0], sibling)
-
-    def relay(k):
-        far = msg.at[k, 1 - side, core]
-        arrived(far, x_send.at[k], x_recv.at[k], across)
-        send(far, far, s_send.at[k, 1], s_recv.at[k, 1], sibling)
-
-    def gather_end(k):
-        arrived(msg.at[k, side, 1 - core], s_send.at[k, 0], s_recv.at[k, 0], sibling)
-        arrived(msg.at[k, 1 - side, 1 - core], s_send.at[k, 1], s_recv.at[k, 1], sibling)
-
-    def gather_rows(k):
-        mine = lax.broadcasted_iota(jnp.int32, (rows, LANES), 1) == me
+            arrived(own, z_send.at[kind, k], z_recv.at[kind, k], in_plane(k))
+        send(own, own, x_send.at[kind, k], x_recv.at[kind, k], across)
+        send(own, own, s_send.at[kind, k, 0], s_recv.at[kind, k, 0], sibling)
+
+    def relay(kind, k):
+        far = msg.at[kind, k, 1 - side, core]
+        arrived(far, x_send.at[kind, k], x_recv.at[kind, k], across)
+        send(far, far, s_send.at[kind, k, 1], s_recv.at[kind, k, 1], sibling)
+
+    def gather(kind, k):
+        for i, s in enumerate((side, 1 - side)):
+            arrived(
+                msg.at[kind, k, s, 1 - core],
+                s_send.at[kind, k, i], s_recv.at[kind, k, i], sibling,
+            )
+        place = lax.broadcasted_iota(jnp.int32, (rows, LANES), 1)
         at = k * chunk
+        target = (x_ref, eg_ref)[kind]
         for s in range(2):
-            ins, grads = [], []
+            left, right = [], []
             for c in range(2):
-                extra = msg[k, s, c, :, wide:].astype(jnp.float32)
-                dense_w = extra[:rows, :LANES] + extra[:rows, LANES:] + extra[rows:, :LANES]
-                weight = jnp.sum(jnp.where(mine, dense_w, 0.0), axis=1, keepdims=True)
-                mask = jnp.sum(jnp.where(mine, extra[rows:, LANES:], 0.0), axis=1, keepdims=True)
-                body = msg[k, s, c, :, :wide].astype(jnp.float32)
-                ins.append(body[:rows] * mask)
-                grads.append(body[rows:] * weight)
-                first = at + (2 * s + c) * rows
-                scale[first:first + rows, :] = jnp.broadcast_to(weight, (rows, LANES))
+                extra = msg[kind, k, s, c, :, half:].astype(jnp.float32)
+                if kind == 0:
+                    kept = jnp.where(place == me, extra[:rows], 0.0)
+                else:
+                    kept = jnp.where(place % (LANES // 2) == me, extra[:rows], 0.0)
+                    kept = kept + jnp.where(place == me, extra[rows:], 0.0)
+                factor = jnp.sum(kept, axis=1, keepdims=True)
+                body = msg[kind, k, s, c, :, :half].astype(jnp.float32)
+                left.append(body[:rows] * factor)
+                right.append(body[rows:] * factor)
+                if kind == 1:
+                    first = at + (2 * s + c) * rows
+                    scale[first:first + rows, :] = jnp.broadcast_to(factor, (rows, LANES))
             here = slice(at + 2 * s * rows, at + 2 * (s + 1) * rows)
-            x_ref[here, :] = jnp.concatenate(ins, axis=0).astype(jnp.bfloat16)
-            eg_ref[here, :] = jnp.concatenate(grads, axis=0).astype(jnp.bfloat16)
+            target[here, :half] = jnp.concatenate(left, axis=0).astype(jnp.bfloat16)
+            target[here, half:] = jnp.concatenate(right, axis=0).astype(jnp.bfloat16)
 
     def first_half(g, hooks):
         tile = ff
@@ -254,6 +265,8 @@
             give(i)
             for hook in hooks[i]:
                 hook()
+        for k in range(g * per, (g + 1) * per):
+            gather(1, k)
         if g == 0:
             loads[6].wait()
 
@@ -268,7 +281,6 @@
         for hook in hooks[2]:
             hook()
 
-    half = wide // 2
     tile_out = min(512, half)
 
     def give_back(kind, g, product):
@@ -343,27 +355,39 @@
             total = total + last_z[kind, k].astype(jnp.float32)
         sum_ref[kind] = total.astype(jnp.bfloat16)
 
-    own = msg.at[0, side, core]
-    spread(0)
-    for k in range(1, planes):
-        send(own, msg.at[k, side, core], z_send.at[k], z_recv.at[k], in_plane(k))
-
+    for k in range(planes):
+        for kind in range(2):
+            if k == 0:
+                spread(kind, 0)
+            else:
+                send(
+                    msg.at[kind, 0, side, core], msg.at[kind, k, side, core],
+                    z_send.at[kind, k], z_recv.at[kind, k], in_plane(k),
+                )
     for k in range(per):
-        relay(k)
+        relay(0, k)
         if k + 1 < per:
-            spread(k + 1)
+            spread(0, k + 1)
     for g in range(groups):
-        for k in range(g * per, (g + 1) * per):
-            gather_end(k)
-            gather_rows(k)
+        now = range(g * per, (g + 1) * per)
+        coming = range((g + 1) * per, (g + 2) * per) if g + 1 < groups else ()
+        for k in now:
+            gather(0, k)
         hooks = [[], [], []]
-        if g + 1 < groups:
-            coming = range((g + 1) * per, (g + 2) * per)
-            hooks[0] = [functools.partial(spread, coming[0])]
-            hooks[1] = [functools.partial(spread, k) for k in coming[1:]]
-            hooks[1].append(functools.partial(relay, coming[0]))
-            hooks[2] = [functools.partial(relay, k) for k in coming[1:]]
+        if g == 0:
+            for k in now:
+                hooks[0].append(functools.partial(relay, 1, k))
+                if k + 1 < per:
+                    hooks[0].append(functools.partial(spread, 1, k + 1))
+        else:
+            hooks[0] += [functools.partial(relay, 1, k) for k in now]
+        for k in coming:
+            hooks[1].append(functools.partial(spread, 0, k))
+        for k in coming:
+            hooks[2].append(functools.partial(relay, 0, k))
+            hooks[2].append(functools.partial(spread, 1, k))
         first_half(g, hooks)
+
     step = min(256, wide)
 
     def down_grad():
@@ -448,7 +472,7 @@
             pltpu.VMEM((wide, ff), bf16),
             pltpu.VMEM((ff, wide), bf16),
             dma((7,)),
-            pltpu.VMEM((planes, 2, 2, 2 * rows, wide + 2 * LANES), bf16),
+            pltpu.VMEM((2, planes, 2, 2, 2 * rows, wide // 2 + LANES), bf16),
             pltpu.VMEM((total, LANES), jnp.float32),
             pltpu.VMEM((groups, 3, per * chunk, ff), bf16),
             pltpu.VMEM((groups, 3, per * chunk, ff), bf16),
@@ -458,9 +482,9 @@
             pltpu.VMEM((2, groups, per, 2 * rows, wide // 2), bf16),
             pltpu.VMEM((2, groups, per, 2 * rows, wide // 2), bf16),
             pltpu.VMEM((2, planes, 2 * rows, wide // 2), bf16),
-            dma((planes,)), dma((planes,)),
-            dma((planes,)), dma((planes,)),
-            dma((planes, 2)), dma((planes, 2)),
+            dma((2, planes)), dma((2, planes)),
+            dma((2, planes)), dma((2, planes)),
+            dma((2, planes, 2)), dma((2, planes, 2)),
             dma((groups, 3)), dma((groups, 3)),
             dma((2, groups)), dma((2, groups)),
             dma((2, groups)), dma((2, groups)),
@@ -533,7 +557,7 @@
         and experts % 4 == 0
         and planes & (planes - 1) == 0
         and planes <= 4
-        and experts <= LANES
+        and experts <= LANES // 2
         and tokens.shape[0] % 8 == 0
     )
     if not fits:

time: 48.4 us -> 50.7 us (1.048)
  Pallas kernels: 47.7 us -> 49.9 us
    pallas_call x1, Pallas kernels: 43.3 us -> 45.5 us  [exchange(): pl.pallas_call(functools.partial(exchange_kernel, planes, per), out_shape...]
where the time goes in v6:
time: 50.7 us; the launch traced here: 50.5 us
  Pallas kernels  49.9 us (98%)
  between operations  0.64 us (1%)
    pallas_call x1, Pallas kernels, exchange(): pl.pallas_call(functools.partial(exchange_kernel, planes, per), out_shape...  45.5 us
    pallas_call x1, Pallas kernels, store(): pl.pallas_call(store_kernel, out_shape=(jax.ShapeDtypeStruct((rows, wide)...  4.35 us

profile of v6, /device:TPU:0, one launch (start us, length us, event | category | flops | bytes accessed | tf_op | source)
XLA Modules:
  0.0 50.5 jit_solution(8356302266708964443)
XLA Ops:
  0.6 45.5 %exchange.1 = (bf16[2,16,1024]{2,1,0:T(8,128)(2,1)S(1)}, bf16[2048,768]{1,0:T(8,128)(2,1)S(1)}, bf16[2048,768]{1,0:T(8,128)(2,1)S(1)}, bf16[768,2048]{1,0:T(8,128)(2,1)S(1)}) custom-call(bf16[8,2048]{1,0:T(8,128)(2,1)} %tok_hbm.1, bf16[8,2048]{1,0:T(8,128)(2,1)} %grad_hbm.1, s32[8,8]{1,0:T(8,128)} %id_hbm.1, f32[8,8]{1,0:T(8,128)} %weight_hbm.1, ...), custom_call_target="tpu_custom_call" | custom-call | tf_op jit(solution)/shard_map/exchange/pallas_call | solution.py:451
  46.2 4.3 %store.1 = (bf16[8,2048]{1,0:T(8,128)(2,1)}, bf16[8,2048]{1,0:T(8,128)(2,1)}, bf16[1,2048,768]{2,1,0:T(8,128)(2,1)}, bf16[1,2048,768]{2,1,0:T(8,128)(2,1)}, bf16[1,768,2048]{2,1,0:T(8,128)(2,1)}) custom-call(bf16[2,16,1024]{2,1,0:T(8,128)(2,1)S(1)} %get-tuple-element.9.sum_ref, bf16[2048,768]{1,0:T(8,128)(2,1)S(1)} %get-tuple-element.10.gate_in, ...), custom_call_target="tpu_custom_call" | custom-call | tf_op jit(solution)/shard_map/store/pallas_call | solution.py:535

commit v7 on v5

--- a/solution.py
+++ b/solution.py
@@ -348,10 +348,12 @@
     for k in range(1, planes):
         send(own, msg.at[k, side, core], z_send.at[k], z_recv.at[k], in_plane(k))
 
+    if per > 1:
+        spread(1)
     for k in range(per):
         relay(k)
-        if k + 1 < per:
-            spread(k + 1)
+        if k + 2 < per:
+            spread(k + 2)
     for g in range(groups):
         for k in range(g * per, (g + 1) * per):
             gather_end(k)
@@ -392,18 +394,22 @@
 
     for g in range(groups):
         outputs(g)
+        if g == groups - 1 and g == 0:
+            sum_core(0, g)
         if g > 0:
             sum_core(1, g - 1)
             sum_side(0, g - 1)
+        if g == groups - 1:
+            down_grad()
         inputs(g)
         if g > 0:
             sum_side(1, g - 1)
-        sum_core(0, g)
+        if groups > 1:
+            sum_core(0, g)
     sum_core(1, groups - 1)
     sum_side(0, groups - 1)
-    down_grad()
+    in_grads(0)
     sum_side(1, groups - 1)
-    in_grads(0)
     in_grads(1)
     finish(0)
     finish(1)
@@ -419,7 +425,7 @@
     total = experts * rows
     chunk = 4 * rows
     bf16 = jnp.bfloat16
-    per = max(1, planes // 2)
+    per = planes
     groups = planes // per
     vmem = pl.BlockSpec(memory_space=pltpu.VMEM)
     hbm = pl.BlockSpec(memory_space=pltpu.HBM)

time: 48.4 us -> 52.7 us (1.089)
  Pallas kernels: 47.7 us -> 51.9 us
    pallas_call x1, Pallas kernels: 43.3 us -> 47.6 us  [exchange(): pl.pallas_call(functools.partial(exchange_kernel, planes, per), out_shape...]
where the time goes in v7:
time: 52.7 us; the launch traced here: 52.6 us
  Pallas kernels  51.9 us (98%)
  between operations  0.64 us (1%)
    pallas_call x1, Pallas kernels, exchange(): pl.pallas_call(functools.partial(exchange_kernel, planes, per), out_shape...  47.6 us
    pallas_call x1, Pallas kernels, store(): pl.pallas_call(store_kernel, out_shape=(jax.ShapeDtypeStruct((rows, wide)...  4.35 us

profile of v7, /device:TPU:0, one launch (start us, length us, event | category | flops | bytes accessed | tf_op | source)
XLA Modules:
  0.0 52.6 jit_solution(3154365520504055736)
XLA Ops:
  0.6 47.6 %exchange.1 = (bf16[2,16,1024]{2,1,0:T(8,128)(2,1)S(1)}, bf16[2048,768]{1,0:T(8,128)(2,1)S(1)}, bf16[2048,768]{1,0:T(8,128)(2,1)S(1)}, bf16[768,2048]{1,0:T(8,128)(2,1)S(1)}) custom-call(bf16[8,2048]{1,0:T(8,128)(2,1)} %tok_hbm.1, bf16[8,2048]{1,0:T(8,128)(2,1)} %grad_hbm.1, s32[8,8]{1,0:T(8,128)} %id_hbm.1, f32[8,8]{1,0:T(8,128)} %weight_hbm.1, ...), custom_call_target="tpu_custom_call" | custom-call | tf_op jit(solution)/shard_map/exchange/pallas_call | solution.py:433
  48.2 4.3 %store.1 = (bf16[8,2048]{1,0:T(8,128)(2,1)}, bf16[8,2048]{1,0:T(8,128)(2,1)}, bf16[1,2048,768]{2,1,0:T(8,128)(2,1)}, bf16[1,2048,768]{2,1,0:T(8,128)(2,1)}, bf16[1,768,2048]{2,1,0:T(8,128)(2,1)}) custom-call(bf16[2,16,1024]{2,1,0:T(8,128)(2,1)S(1)} %get-tuple-element.9.sum_ref, bf16[2048,768]{1,0:T(8,128)(2,1)S(1)} %get-tuple-element.10.gate_in, ...), custom_call_target="tpu_custom_call" | custom-call | tf_op jit(solution)/shard_map/store/pallas_call | solution.py:517
